TPU v7x, 256 devices: a whole 4x4x8 slice. The times are simulated.
256 devices in a mesh: dp: 8 (over x, core), mp: 32 (over y, z).
Axes of the slice: x: 4, y: 4, z: 8, core: 2. Of those that a mesh axis runs over, the one named last changes fastest.
Arguments:
- x_in: bfloat16 [4096, 12288], P('dp', 'mp'), may hold values from -0.25 to 0.25
- grad_pre: bfloat16 [4096, 24576], P('dp', 'mp'), may hold values from -6 to 6
- weight_blocks: bfloat16 [4096, 128, 128], P('mp'), may hold values from -0.125 to 0.125
- slot_row: int32 [4096], P('mp'), may hold values from 0 to 2
- slot_col: int32 [4096], P('mp'), may hold values from 0 to 191, as said below
- slot_count: int32 [32], P('mp'), may hold values from 32 to 128, as said below
Outputs:
- grad_x: bfloat16 [4096, 12288], P('dp', 'mp')
- grad_blocks: float32 [4096, 128, 128], P('mp', 'dp')
Inputs may be any that keep to these rules, and one draw needn't show every extreme that they name: `slot_col`: of each owner's 128 slots the first slot_count are live and name distinct (row, column) pairs; the rest hold indices in range and are ignored. The live slots of one owner name at most 2 distinct block-columns among the 6 block-columns c with c // 6 equal to any one index of mp, and one owner names exactly 2 of every such range. `slot_count`: some owner fills all of its slots.
All inputs are finite; a program needn't handle non-finite values.
Results may differ from a plain program's by a relative error of at most 0.001.
Values may be sent and summed in bfloat16 or wider, within the bound.
No kernel may reach another device: no remote copies, remote signals or barrier semaphores. Data moves between devices by JAX's collectives and lax.ppermute only.
A program may use at most 192 MiB of HBM per device.

v0:
```python
import jax
import jax.numpy as jnp
from jax import lax
from jax.sharding import PartitionSpec as P


def on_device(x_in, grad_pre, weight_blocks, slot_row, slot_col, slot_count):
    high = lax.Precision.HIGHEST
    tokens = x_in.shape[0]
    block = weight_blocks.shape[1]
    slots = weight_blocks.shape[0]
    owners = lax.axis_size("mp")
    row_blocks = x_in.shape[1] // block
    col_blocks = grad_pre.shape[1] // block
    alive = jnp.arange(slots) < slot_count[0]
    whole = lax.all_gather(grad_pre, "mp", axis=1, tiled=True)
    source = whole.reshape(tokens, owners * col_blocks, block)
    x_three = x_in.reshape(tokens, row_blocks, block)
    groups = slots // 16
    items = (
        slot_row.reshape(groups, 16),
        slot_col.reshape(groups, 16),
        weight_blocks.reshape(groups, 16, block, block),
        alive.reshape(groups, 16),
    )

    def advance(total, item):
        rows, picks, weights, live_now = item
        mask = live_now.astype(jnp.float32)
        x_blocks = jnp.take(x_three, rows, axis=1)
        p_blocks = jnp.take(source, picks, axis=1)
        grads = (
            jnp.einsum("tgj,tgk->gjk", x_blocks, p_blocks, preferred_element_type=jnp.float32)
            * mask[:, None, None]
        )
        contrib = jnp.einsum("tgk,gjk->tgj", p_blocks, weights, preferred_element_type=jnp.float32)
        place = (rows[:, None] == jnp.arange(row_blocks)[None, :]).astype(jnp.float32) * mask[
            :, None
        ]
        total = total + jnp.einsum("tgj,gr->trj", contrib, place, precision=high)
        return (total, grads)

    start_total = jnp.zeros((tokens, row_blocks, block), jnp.float32)
    total, grads = lax.scan(advance, start_total, items)
    grads = grads.reshape(slots, block, block)
    shares = lax.psum_scatter(grads, "dp", scatter_dimension=1, tiled=True)
    return (total.reshape(tokens, row_blocks * block).astype(jnp.bfloat16), shares)


def solution(mesh):
    placed = (P("dp", "mp"), P("dp", "mp"), P("mp", None, None), P("mp"), P("mp"), P("mp"))
    return jax.shard_map(
        on_device,
        mesh=mesh,
        in_specs=placed,
        out_specs=(P("dp", "mp"), P("mp", "dp", None)),
        check_vma=False,
    )
```

profile of v0, /device:TPU:1, one launch (start us, length us, event | category | flops | bytes accessed | tf_op | source)
XLA Modules:
  0.0 546.2 jit_solution(8578026056576515761)
XLA Ops:
  11.5 186.9 %all-gather.2.cloned.1.call-done = bf16[512,24576]{0,1:T(8,128)(2,1)} async-done(((bf16[512,768]{0,1:T(8,128)(2,1)}), bf16[512,24576]{0,1:T(8,128)(2,1)}) %all-gather.2.cloned.1.call-update) | async-done | bytes 25165840 | tf_op jit(solution)/shard_map/all_gather | solution.py:16
  198.4 30.9 %copy.19 = bf16[512,192,128]{2,0,1:T(8,128)(2,1)} copy(bf16[512,192,128]{0,2,1:T(8,128)(2,1)} %bitcast.83) | data formatting | bytes 50331648
  229.3 258.0 %while.13 = (s32[]{:T(128)}, f32[512,3,128]{2,1,0:T(4,128)S(1)}, f32[8,16,128,128]{3,2,1,0:T(8,128)}, s32[8,16]{1,0:T(8,128)S(1)}, pred[8,16]{1,0:T(8,128)(4,1)}...) while((s32[]{:T(128)}, f32[512,3,128]{2,1,0:T(4,128)S(1)}, ...), condition=%wide.region_1.2_spmd.clone, body=%wide.region_0.1_spmd.clone.sunk | while | flops 578423168 | bytes 34622208 | solution.py:44
  229.9 9.1 %gather_fusion = bf16[16,512,128]{2,1,0:T(8,128)(2,1)S(1)} fusion(bf16[512,192,128]{2,0,1:T(8,128)(2,1)} %get-tuple-element.221, s32[1024]{0:T(1024)S(1)} %pad_clamp_fusion.4), kind=kCustom, calls=%fused_computation.clone.clone.1 | custom fusion | bytes 4194368 | tf_op jit(solution)/shard_map/while/body/eval_jaxpr/jit(_take)/gather | solution.py:31
  250.5 5.4 copy.25
  255.9 5.6 %fusion.58 = f32[512,3,128]{2,1,0:T(4,128)S(1)} fusion(f32[512,16,128]{2,1,0:T(8,128)} %copy.25, f32[512,3,128]{2,1,0:T(4,128)S(1)} %get-tuple-element.204, pred[]{:T(512)S(6)} %compare.3, f32[16]{0:T(128)S(1)} %fusion.57, s32[16]{0:T(128)S(1)} %get-tuple-element.189), kind=kOutput, calls=%fused_computation.11.clone.1 | convolution fusion | flops 38142048 | bytes 5767297 | tf_op jit(solution)/shard_map/while/body/eval_jaxpr/tgj,gr->trj/dot_general | solution.py:40
  262.2 9.1 %gather_fusion = bf16[16,512,128]{2,1,0:T(8,128)(2,1)S(1)} fusion(bf16[512,192,128]{2,0,1:T(8,128)(2,1)} %get-tuple-element.221, s32[1024]{0:T(1024)S(1)} %pad_clamp_fusion.4), kind=kCustom, calls=%fused_computation.clone.clone.1 | custom fusion | bytes 4194368 | tf_op jit(solution)/shard_map/while/body/eval_jaxpr/jit(_take)/gather | solution.py:31
  282.8 5.4 copy.25
  288.2 5.6 %fusion.58 = f32[512,3,128]{2,1,0:T(4,128)S(1)} fusion(f32[512,16,128]{2,1,0:T(8,128)} %copy.25, f32[512,3,128]{2,1,0:T(4,128)S(1)} %get-tuple-element.204, pred[]{:T(512)S(6)} %compare.3, f32[16]{0:T(128)S(1)} %fusion.57, s32[16]{0:T(128)S(1)} %get-tuple-element.189), kind=kOutput, calls=%fused_computation.11.clone.1 | convolution fusion | flops 38142048 | bytes 5767297 | tf_op jit(solution)/shard_map/while/body/eval_jaxpr/tgj,gr->trj/dot_general | solution.py:40
  294.4 9.1 %gather_fusion = bf16[16,512,128]{2,1,0:T(8,128)(2,1)S(1)} fusion(bf16[512,192,128]{2,0,1:T(8,128)(2,1)} %get-tuple-element.221, s32[1024]{0:T(1024)S(1)} %pad_clamp_fusion.4), kind=kCustom, calls=%fused_computation.clone.clone.1 | custom fusion | bytes 4194368 | tf_op jit(solution)/shard_map/while/body/eval_jaxpr/jit(_take)/gather | solution.py:31
  315.0 5.4 copy.25
  320.4 5.6 %fusion.58 = f32[512,3,128]{2,1,0:T(4,128)S(1)} fusion(f32[512,16,128]{2,1,0:T(8,128)} %copy.25, f32[512,3,128]{2,1,0:T(4,128)S(1)} %get-tuple-element.204, pred[]{:T(512)S(6)} %compare.3, f32[16]{0:T(128)S(1)} %fusion.57, s32[16]{0:T(128)S(1)} %get-tuple-element.189), kind=kOutput, calls=%fused_computation.11.clone.1 | convolution fusion | flops 38142048 | bytes 5767297 | tf_op jit(solution)/shard_map/while/body/eval_jaxpr/tgj,gr->trj/dot_general | solution.py:40
  326.7 9.1 %gather_fusion = bf16[16,512,128]{2,1,0:T(8,128)(2,1)S(1)} fusion(bf16[512,192,128]{2,0,1:T(8,128)(2,1)} %get-tuple-element.221, s32[1024]{0:T(1024)S(1)} %pad_clamp_fusion.4), kind=kCustom, calls=%fused_computation.clone.clone.1 | custom fusion | bytes 4194368 | tf_op jit(solution)/shard_map/while/body/eval_jaxpr/jit(_take)/gather | solution.py:31
  347.3 5.4 copy.25
  352.7 5.6 %fusion.58 = f32[512,3,128]{2,1,0:T(4,128)S(1)} fusion(f32[512,16,128]{2,1,0:T(8,128)} %copy.25, f32[512,3,128]{2,1,0:T(4,128)S(1)} %get-tuple-element.204, pred[]{:T(512)S(6)} %compare.3, f32[16]{0:T(128)S(1)} %fusion.57, s32[16]{0:T(128)S(1)} %get-tuple-element.189), kind=kOutput, calls=%fused_computation.11.clone.1 | convolution fusion | flops 38142048 | bytes 5767297 | tf_op jit(solution)/shard_map/while/body/eval_jaxpr/tgj,gr->trj/dot_general | solution.py:40
  359.0 9.1 %gather_fusion = bf16[16,512,128]{2,1,0:T(8,128)(2,1)S(1)} fusion(bf16[512,192,128]{2,0,1:T(8,128)(2,1)} %get-tuple-element.221, s32[1024]{0:T(1024)S(1)} %pad_clamp_fusion.4), kind=kCustom, calls=%fused_computation.clone.clone.1 | custom fusion | bytes 4194368 | tf_op jit(solution)/shard_map/while/body/eval_jaxpr/jit(_take)/gather | solution.py:31
  385.0 5.6 %fusion.58 = f32[512,3,128]{2,1,0:T(4,128)S(1)} fusion(f32[512,16,128]{2,1,0:T(8,128)} %copy.25, f32[512,3,128]{2,1,0:T(4,128)S(1)} %get-tuple-element.204, pred[]{:T(512)S(6)} %compare.3, f32[16]{0:T(128)S(1)} %fusion.57, s32[16]{0:T(128)S(1)} %get-tuple-element.189), kind=kOutput, calls=%fused_computation.11.clone.1 | convolution fusion | flops 38142048 | bytes 5767297 | tf_op jit(solution)/shard_map/while/body/eval_jaxpr/tgj,gr->trj/dot_general | solution.py:40
  391.2 9.1 %gather_fusion = bf16[16,512,128]{2,1,0:T(8,128)(2,1)S(1)} fusion(bf16[512,192,128]{2,0,1:T(8,128)(2,1)} %get-tuple-element.221, s32[1024]{0:T(1024)S(1)} %pad_clamp_fusion.4), kind=kCustom, calls=%fused_computation.clone.clone.1 | custom fusion | bytes 4194368 | tf_op jit(solution)/shard_map/while/body/eval_jaxpr/jit(_take)/gather | solution.py:31
  417.1 5.6 %fusion.58 = f32[512,3,128]{2,1,0:T(4,128)S(1)} fusion(f32[512,16,128]{2,1,0:T(8,128)} %copy.25, f32[512,3,128]{2,1,0:T(4,128)S(1)} %get-tuple-element.204, pred[]{:T(512)S(6)} %compare.3, f32[16]{0:T(128)S(1)} %fusion.57, s32[16]{0:T(128)S(1)} %get-tuple-element.189), kind=kOutput, calls=%fused_computation.11.clone.1 | convolution fusion | flops 38142048 | bytes 5767297 | tf_op jit(solution)/shard_map/while/body/eval_jaxpr/tgj,gr->trj/dot_general | solution.py:40
  423.4 9.1 %gather_fusion = bf16[16,512,128]{2,1,0:T(8,128)(2,1)S(1)} fusion(bf16[512,192,128]{2,0,1:T(8,128)(2,1)} %get-tuple-element.221, s32[1024]{0:T(1024)S(1)} %pad_clamp_fusion.4), kind=kCustom, calls=%fused_computation.clone.clone.1 | custom fusion | bytes 4194368 | tf_op jit(solution)/shard_map/while/body/eval_jaxpr/jit(_take)/gather | solution.py:31
  449.4 5.6 %fusion.58 = f32[512,3,128]{2,1,0:T(4,128)S(1)} fusion(f32[512,16,128]{2,1,0:T(8,128)} %copy.25, f32[512,3,128]{2,1,0:T(4,128)S(1)} %get-tuple-element.204, pred[]{:T(512)S(6)} %compare.3, f32[16]{0:T(128)S(1)} %fusion.57, s32[16]{0:T(128)S(1)} %get-tuple-element.189), kind=kOutput, calls=%fused_computation.11.clone.1 | convolution fusion | flops 38142048 | bytes 5767297 | tf_op jit(solution)/shard_map/while/body/eval_jaxpr/tgj,gr->trj/dot_general | solution.py:40
  455.7 9.1 %gather_fusion = bf16[16,512,128]{2,1,0:T(8,128)(2,1)S(1)} fusion(bf16[512,192,128]{2,0,1:T(8,128)(2,1)} %get-tuple-element.221, s32[1024]{0:T(1024)S(1)} %pad_clamp_fusion.4), kind=kCustom, calls=%fused_computation.clone.clone.1 | custom fusion | bytes 4194368 | tf_op jit(solution)/shard_map/while/body/eval_jaxpr/jit(_take)/gather | solution.py:31
  481.7 5.6 %fusion.58 = f32[512,3,128]{2,1,0:T(4,128)S(1)} fusion(f32[512,16,128]{2,1,0:T(8,128)} %copy.25, f32[512,3,128]{2,1,0:T(4,128)S(1)} %get-tuple-element.204, pred[]{:T(512)S(6)} %compare.3, f32[16]{0:T(128)S(1)} %fusion.57, s32[16]{0:T(128)S(1)} %get-tuple-element.189), kind=kOutput, calls=%fused_computation.11.clone.1 | convolution fusion | flops 38142048 | bytes 5767297 | tf_op jit(solution)/shard_map/while/body/eval_jaxpr/tgj,gr->trj/dot_general | solution.py:40
  488.5 50.9 %reduce-scatter.2.cloned.1.call-done = f32[128,16,128]{2,1,0:T(8,128)} async-done(((f32[128,128,128]{2,1,0:T(8,128)}), f32[128,16,128]{2,1,0:T(8,128)}) %reduce-scatter.2.cloned.1.call-update) | async-done | bytes 1048592 | tf_op jit(solution)/shard_map/reduce_scatter | solution.py:46
  (152 shorter events, 122.9 us)
Async XLA Ops:
  7.2 2.5 copy-start
  7.2 2.9 copy-start.5
  7.2 3.0 copy-start.6
  7.2 191.2 %all-gather.2.cloned.1.call-start = ((), (), s32[]{:S(2)}) async-start(), calls=%async_computation.1 | async-start | bytes 25952256 | tf_op jit(solution)/shard_map/all_gather | solution.py:16
  9.6 529.8 %reduce-scatter.2.cloned.1.call-start = ((), (), s32[]{:S(2)}) async-start(), calls=%async_computation.2 | async-start | bytes 9437184 | tf_op jit(solution)/shard_map/reduce_scatter | solution.py:46
  229.3 0.6 copy-start.3
  255.9 5.6 %copy-start.2 = (s32[8,16]{1,0:T(8,128)S(1)}, s32[8,16]{1,0:T(8,128)}, u32[]{:S(2)}) copy-start(s32[8,16]{1,0:T(8,128)} %copy-done.1) | copy-start | bytes 1540 | tf_op jit(solution)/shard_map/while
  255.9 5.6 %copy-start.4 = (s32[8,16]{1,0:T(8,128)S(1)}, s32[8,16]{1,0:T(8,128)}, u32[]{:S(2)}) copy-start(s32[8,16]{1,0:T(8,128)} %copy-done.3) | copy-start | bytes 1540 | tf_op jit(solution)/shard_map/while
  261.6 0.6 copy-start.1
  288.2 5.6 %copy-start.2 = (s32[8,16]{1,0:T(8,128)S(1)}, s32[8,16]{1,0:T(8,128)}, u32[]{:S(2)}) copy-start(s32[8,16]{1,0:T(8,128)} %copy-done.1) | copy-start | bytes 1540 | tf_op jit(solution)/shard_map/while
  288.2 5.6 %copy-start.4 = (s32[8,16]{1,0:T(8,128)S(1)}, s32[8,16]{1,0:T(8,128)}, u32[]{:S(2)}) copy-start(s32[8,16]{1,0:T(8,128)} %copy-done.3) | copy-start | bytes 1540 | tf_op jit(solution)/shard_map/while
  320.4 5.6 %copy-start.2 = (s32[8,16]{1,0:T(8,128)S(1)}, s32[8,16]{1,0:T(8,128)}, u32[]{:S(2)}) copy-start(s32[8,16]{1,0:T(8,128)} %copy-done.1) | copy-start | bytes 1540 | tf_op jit(solution)/shard_map/while
  320.4 5.6 %copy-start.4 = (s32[8,16]{1,0:T(8,128)S(1)}, s32[8,16]{1,0:T(8,128)}, u32[]{:S(2)}) copy-start(s32[8,16]{1,0:T(8,128)} %copy-done.3) | copy-start | bytes 1540 | tf_op jit(solution)/shard_map/while
  352.7 5.6 %copy-start.2 = (s32[8,16]{1,0:T(8,128)S(1)}, s32[8,16]{1,0:T(8,128)}, u32[]{:S(2)}) copy-start(s32[8,16]{1,0:T(8,128)} %copy-done.1) | copy-start | bytes 1540 | tf_op jit(solution)/shard_map/while
  352.7 5.6 %copy-start.4 = (s32[8,16]{1,0:T(8,128)S(1)}, s32[8,16]{1,0:T(8,128)}, u32[]{:S(2)}) copy-start(s32[8,16]{1,0:T(8,128)} %copy-done.3) | copy-start | bytes 1540 | tf_op jit(solution)/shard_map/while
  358.4 0.6 copy-start.1
  385.0 5.6 %copy-start.2 = (s32[8,16]{1,0:T(8,128)S(1)}, s32[8,16]{1,0:T(8,128)}, u32[]{:S(2)}) copy-start(s32[8,16]{1,0:T(8,128)} %copy-done.1) | copy-start | bytes 1540 | tf_op jit(solution)/shard_map/while
  385.0 5.6 %copy-start.4 = (s32[8,16]{1,0:T(8,128)S(1)}, s32[8,16]{1,0:T(8,128)}, u32[]{:S(2)}) copy-start(s32[8,16]{1,0:T(8,128)} %copy-done.3) | copy-start | bytes 1540 | tf_op jit(solution)/shard_map/while
  417.1 5.6 %copy-start.2 = (s32[8,16]{1,0:T(8,128)S(1)}, s32[8,16]{1,0:T(8,128)}, u32[]{:S(2)}) copy-start(s32[8,16]{1,0:T(8,128)} %copy-done.1) | copy-start | bytes 1540 | tf_op jit(solution)/shard_map/while
  417.1 5.6 %copy-start.4 = (s32[8,16]{1,0:T(8,128)S(1)}, s32[8,16]{1,0:T(8,128)}, u32[]{:S(2)}) copy-start(s32[8,16]{1,0:T(8,128)} %copy-done.3) | copy-start | bytes 1540 | tf_op jit(solution)/shard_map/while
  449.4 5.6 %copy-start.2 = (s32[8,16]{1,0:T(8,128)S(1)}, s32[8,16]{1,0:T(8,128)}, u32[]{:S(2)}) copy-start(s32[8,16]{1,0:T(8,128)} %copy-done.1) | copy-start | bytes 1540 | tf_op jit(solution)/shard_map/while
  449.4 5.6 %copy-start.4 = (s32[8,16]{1,0:T(8,128)S(1)}, s32[8,16]{1,0:T(8,128)}, u32[]{:S(2)}) copy-start(s32[8,16]{1,0:T(8,128)} %copy-done.3) | copy-start | bytes 1540 | tf_op jit(solution)/shard_map/while
  481.7 5.6 %copy-start.2 = (s32[8,16]{1,0:T(8,128)S(1)}, s32[8,16]{1,0:T(8,128)}, u32[]{:S(2)}) copy-start(s32[8,16]{1,0:T(8,128)} %copy-done.1) | copy-start | bytes 1540 | tf_op jit(solution)/shard_map/while
  481.7 5.6 %copy-start.4 = (s32[8,16]{1,0:T(8,128)S(1)}, s32[8,16]{1,0:T(8,128)}, u32[]{:S(2)}) copy-start(s32[8,16]{1,0:T(8,128)} %copy-done.3) | copy-start | bytes 1540 | tf_op jit(solution)/shard_map/while
  (13 other events, 7.7 us)
Sparse Core Ops, SparseCore 0:
  11.2 187.1 all-gather.1
  487.5 51.8 reduce-scatter.1
where the time goes:
time: 549 us; the launch traced here: 546 us
  waiting for transfers between devices  238 us (43%)
  local copies, waits for them, and re-layouts  173 us (32%)
  matrix products  104 us (19%)
  other arithmetic  16.2 us (3%)
  between operations  14.8 us (3%)
    all_gather x1, waiting for transfers between devices, on_device(): whole = lax.all_gather(grad_pre, 'mp', axis=1, tiled=True)  187 us
    gather x8, local copies, waits for them, and re-layouts, advance(): p_blocks = jnp.take(source, picks, axis=1)  72.9 us
    reduce_scatter x1, waiting for transfers between devices, on_device(): shares = lax.psum_scatter(grads, 'dp', scatter_dimension=1, tiled=True)  50.9 us
    dot_general x8, matrix products, advance(): total = total + jnp.einsum('tgj,gr->trj', contrib, place, precision=high)  44.8 us
    transpose x8, local copies, waits for them, and re-layouts, advance(): jnp.einsum('tgk,gjk->tgj', p_blocks, weights, preferred_element_type=jnp....  43.5 us
    unnamed x11, local copies, waits for them, and re-layouts  34.6 us
    dot_general x8, matrix products, advance(): jnp.einsum('tgk,gjk->tgj', p_blocks, weights, preferred_element_type=jnp....  30.4 us
    dot_general x8, matrix products, advance(): jnp.einsum('tgj,tgk->gjk', x_blocks, p_blocks, preferred_element_type=jnp...  28.4 us
  transfers between devices with their start and end apart: 2, of which 2 were waited for; matrix products, arithmetic and copies ran while one was open for 0% of the time, Pallas kernels for 0%

commit v1 on v0

v1 whole, which is shorter than its diff:
```python
import jax
import jax.numpy as jnp
from jax import lax
from jax.experimental import pallas as pl
from jax.experimental.pallas import tpu as pltpu
from jax.sharding import PartitionSpec as P

NY, NZ = 4, 8
NX = 4
B = 128
T = 512
CB, RB = 6, 3
D = RB * B
SLOTS = 128
EARLY, LATE = (0, 1, -1, 2, -2), (3, -3, 4)
ORDER = EARLY + LATE
ROUNDS = ((0, 1, -1, 2, -2, 3, -3), (4,))
OWNERS = (1, -1, 2)
DY_PART = (0, 2, 3, 1)
HEAD = 16

VMEM = pl.BlockSpec(memory_space=pltpu.VMEM)
SMEM = pl.BlockSpec(memory_space=pltpu.SMEM)
PARAMS = pltpu.CompilerParams(vmem_limit_bytes=48 << 20)
F32, BF16, I32 = jnp.float32, jnp.bfloat16, jnp.int32


def sds(shape, dtype):
    return jax.ShapeDtypeStruct(shape, dtype)


def cost(flops, moved):
    return pl.CostEstimate(flops=flops, bytes_accessed=moved, transcendentals=0)


def source_column(col):
    src = (col * 43691) >> 18
    return src, col - src * CB


def need_kernel(col, count, need):
    shape = (NY * NZ, SLOTS)
    src, c = source_column(col[...])
    slot = lax.broadcasted_iota(I32, shape, 1)
    hit = (src == lax.broadcasted_iota(I32, shape, 0)) & (slot < count[0])
    lo = jnp.min(jnp.where(hit, c, CB), axis=1, keepdims=True)
    hi = jnp.max(jnp.where(hit, c, -1), axis=1, keepdims=True)
    none = hi < 0
    need[...] = jnp.where(slot == 0, jnp.where(none, 0, lo), jnp.where(none, 0, hi))


def need_table(slot_col, slot_count):
    return pl.pallas_call(
        need_kernel,
        out_shape=sds((NY * NZ, SLOTS), I32),
        in_specs=[VMEM, SMEM],
        out_specs=VMEM,
        cost_estimate=cost(0, 1 << 14),
        name="need",
    )(slot_col.reshape(1, SLOTS), slot_count)


def pack_kernel(me, d, row, col, count, need, w, own, b1, b2, b3, held):
    y = me[0] >> 3
    held[...] = jnp.zeros_like(held)

    @pl.loop(0, SLOTS, unroll=4)
    def _(s):
        src, c = source_column(col[s])
        p = jnp.where(c == need[src, 0], 0, 1)
        at = jnp.where(s < count[0], (src - (y << 3)) & (NY * NZ - 1), NY * NZ)
        rows = pl.ds(pl.multiple_of(row[s] * B, B), B)
        held[at, rows, pl.ds(pl.multiple_of(p * B, B), B)] = w[s]

    own[...] = held[:NZ]
    lo = (d[0] & 1) * (NZ // 2)
    for out, t in ((b1, 3), (b2, 1), (b3, 2)):
        out[...] = held[pl.ds(t * NZ + lo, NZ // 2)]


def pack(me, d, slot_row, slot_col, slot_count, need, w):
    part = sds((NZ // 2, D, 2 * B), BF16)
    return pl.pallas_call(
        pack_kernel,
        out_shape=(sds((NZ, D, 2 * B), BF16), part, part, part),
        in_specs=[SMEM] * 6 + [VMEM],
        out_specs=(VMEM,) * 4,
        scratch_shapes=[pltpu.VMEM((NY * NZ + 1, D, 2 * B), BF16)],
        compiler_params=PARAMS,
        cost_estimate=cost(0, 7 << 20),
        name="pack",
    )(me, d, slot_row, slot_col, slot_count, need, w)


def two_columns(g, cols, part, src, sel):
    for p in range(2):
        lanes = pl.ds(pl.multiple_of(cols[part, p * NY * NZ + src] * B, B), B)
        sel[:, p * B : (p + 1) * B] = g[:, lanes]
    return sel[...]


def early_kernel(me, cols, *refs):
    xts, gs, (out, sel) = refs[:4], refs[4:-2], refs[-2:]
    lo = 0
    for part in range(4):
        for i, dz in enumerate(EARLY):
            src = (me[0] & ~(NZ - 1)) + ((me[0] + dz) & (NZ - 1))
            blk = two_columns(gs[i], cols, part, src, sel.at[(part * len(EARLY) + i) % 2])
            out[:, lo : lo + 2 * B] = jnp.dot(xts[part][HEAD:, :], blk, preferred_element_type=F32)
            lo += 2 * B


def early(me, cols, xts, gs):
    width = 4 * 2 * B * len(gs)
    return pl.pallas_call(
        early_kernel,
        out_shape=sds((D, width), F32),
        in_specs=[SMEM] * 2 + [VMEM] * (4 + len(gs)),
        out_specs=VMEM,
        scratch_shapes=[pltpu.VMEM((2, T, 2 * B), BF16)],
        compiler_params=PARAMS,
        cost_estimate=cost(2 * width * T * D, D * width * 4 + len(gs) * T * CB * B * 2 + 8 * T * D),
        name="early",
    )(me, cols, *xts, *gs)


def late_kernel(me, d, cols, *refs):
    xts, gs, (mine, other, turned, sel) = refs[:4], refs[4:-4], refs[-4:]
    half, step = D // 2, RB * 16
    dx, dc = d[0] >> 1, d[0] & 1
    lo = 0
    for part in range(4):
        for cc in range(2):
            for xx in range(NX):
                to = (((dx + xx) & (NX - 1)) << 1) + (dc ^ cc)
                rows = pl.ds(pl.multiple_of(HEAD + to * step, 16), step)
                at = (cc * NX + xx) * step
                turned[at : at + step, :] = xts[part][rows, :]
        for i, dz in enumerate(LATE):
            src = (me[0] & ~(NZ - 1)) + ((me[0] + dz) & (NZ - 1))
            blk = two_columns(gs[i], cols, part, src, sel.at[(part * len(LATE) + i) % 2])
            prod = jnp.dot(turned[...], blk, preferred_element_type=F32)
            mine[:, lo : lo + 2 * B] = prod[:half]
            other[:, lo : lo + 2 * B] = prod[half:]
            lo += 2 * B
    for out in (mine, other):
        out[:, lo:] = jnp.zeros((half, B), F32)


def late(me, d, cols, xts, gs):
    width = 4 * 2 * B * len(gs)
    return pl.pallas_call(
        late_kernel,
        out_shape=(sds((D // 2, width + B), F32),) * 2,
        in_specs=[SMEM] * 3 + [VMEM] * (4 + len(gs)),
        out_specs=(VMEM,) * 2,
        scratch_shapes=[pltpu.VMEM((D, T), BF16), pltpu.VMEM((2, T, 2 * B), BF16)],
        compiler_params=PARAMS,
        cost_estimate=cost(2 * width * T * D, D * width * 4 + len(gs) * T * CB * B * 2 + 8 * T * D),
        name="late",
    )(me, d, cols, *xts, *gs)


def inputs_kernel(stage, first, me, d, cols, own, near, far, *refs):
    gs, refs = refs[: len(stage)], refs[len(stage) :]
    accs, outs, sel = refs[:-5], refs[-5:-1], refs[-1]
    for part in (1, 2, 3, 0):
        total = None if first else accs[part][...]
        for i, dz in enumerate(stage):
            z = (me[0] + dz) & (NZ - 1)
            src = (me[0] & ~(NZ - 1)) + z
            blk = two_columns(gs[i], cols, part, src, sel.at[i % 2])
            if part == 0:
                w = own[z]
            else:
                at = z & (NZ // 2 - 1)
                mine = (z >> 2) == (d[0] & 1)
                w = jnp.where(mine, near[part - 1, at], far[part - 1, at])
            prod = lax.dot_general(blk, w, (((1,), (1,)), ((), ())), preferred_element_type=F32)
            total = prod if total is None else total + prod
        outs[part][...] = total


def inputs(stage, me, d, cols, own, near, far, gs, accs):
    first = not accs
    flops = 4 * 2 * T * D * 2 * B * len(stage)
    return pl.pallas_call(
        lambda *refs: inputs_kernel(stage, first, *refs),
        out_shape=(sds((T, D), F32),) * 4,
        in_specs=[SMEM] * 3 + [VMEM] * (3 + len(gs) + len(accs)),
        out_specs=(VMEM,) * 4,
        scratch_shapes=[pltpu.VMEM((2, T, 2 * B), BF16)],
        compiler_params=PARAMS,
        cost_estimate=cost(flops, 10 << 20),
        name="inputs",
    )(me, d, cols, own, near, far, *gs, *accs)


def turn_kernel(need, x, out):
    n = NY * NZ
    lane = lax.broadcasted_iota(I32, (HEAD, T), 1)
    head = jnp.zeros((HEAD, T), I32)
    for i in range(n):
        head = jnp.where(lane == i, need[i, 0], head)
        head = jnp.where(lane == n + i, need[i, 1], head)
    out[:HEAD, :] = head.astype(F32).astype(BF16)
    held = x[...].T
    for to in range(2 * NX):
        for r in range(RB):
            at = HEAD + (to * RB + r) * 16
            out[at : at + 16, :] = held[r * B + to * 16 : r * B + to * 16 + 16, :]


def turn(need, x):
    return pl.pallas_call(
        turn_kernel,
        out_shape=sds((HEAD + D, T), BF16),
        in_specs=[SMEM, VMEM],
        out_specs=VMEM,
        compiler_params=PARAMS,
        cost_estimate=cost(0, 1 << 20),
        name="turn",
    )(need, x)


def slots_kernel(me, row, col, count, need, *refs):
    ins, out, held = refs[:-2], refs[-2], refs[-1]
    wide = 2 * B
    for part in range(4):
        for i, dz in enumerate(ORDER):
            held[dz & (NZ - 1), part] = ins[part][:, i * wide : (i + 1) * wide]
    y, z = me[0] >> 3, me[0] & 7

    @pl.loop(0, SLOTS, unroll=4)
    def _(s):
        src, c = source_column(col[s])
        p = jnp.where(c == need[src, 0], 0, 1)
        dz = ((src & 7) - z) & (NZ - 1)
        dy = ((src >> 3) - y) & (NY - 1)
        part = jnp.where(dy == 0, DY_PART[0], jnp.where(dy == 1, DY_PART[1], jnp.where(dy == 2, DY_PART[2], DY_PART[3])))
        rows = pl.ds(pl.multiple_of(row[s] * 16, 16), 16)
        lanes = pl.ds(pl.multiple_of(p * B, B), B)
        blk = held[dz, part, rows, lanes]
        out[s] = jnp.where(s < count[0], blk, jnp.zeros_like(blk))


def slots(me, row, col, count, need, parts):
    return pl.pallas_call(
        slots_kernel,
        out_shape=sds((SLOTS, 16, B), F32),
        in_specs=[SMEM] * 5 + [VMEM] * len(parts),
        out_specs=VMEM,
        scratch_shapes=[pltpu.VMEM((NZ, 4, RB * 16, 2 * B), F32)],
        compiler_params=PARAMS,
        cost_estimate=cost(0, 5 << 20),
        name="slots",
    )(me, row, col, count, need, *parts)


def shift_z(k):
    return [(y * NZ + z, y * NZ + (z + k) % NZ) for y in range(NY) for z in range(NZ)]


def shift_y(k):
    return [(y * NZ + z, (y + k) % NY * NZ + z) for y in range(NY) for z in range(NZ)]


def shift_x(k):
    return [(x * 2 + c, (x + k) % NX * 2 + c) for x in range(NX) for c in range(2)]


def tie(*trees):
    return lax.optimization_barrier(trees)


def after(a, first):
    return lax.optimization_barrier((a, first))[0]


def tie(*trees):
    return lax.optimization_barrier(trees)


def on_device(x_in, grad_pre, weight_blocks, slot_row, slot_col, slot_count):
    me = lax.axis_index("mp").astype(I32).reshape(1)
    d = lax.axis_index("dp").astype(I32).reshape(1)
    step = RB * 16

    def z_step(a, k):
        return lax.ppermute(a, "mp", shift_z(k))

    def core_step(a):
        return lax.ppermute(a, "dp", [(a, a ^ 1) for a in range(2 * NX)])

    def y_back(parts):
        return [lax.ppermute(a, "mp", shift_y(k)) for a, k in zip(parts, OWNERS)]

    def pair_step(mine, theirs):
        rows = [mine[i * step : (i + 1) * step] + theirs[i * step : (i + 1) * step] for i in range(NX)]
        top = jnp.max(jnp.abs(mine[step:] + theirs[step:]))
        power = jnp.floor(jnp.log2(2.0**14 / jnp.maximum(top, 1e-30)))
        scale = jnp.exp2(power)
        inside = lax.broadcasted_iota(I32, rows[0].shape, 1) < rows[0].shape[1] - B
        return rows[0], [jnp.where(inside, a * scale, power).astype(jnp.float16) for a in rows[1:]]

    def x_step(out):
        return [lax.ppermute(a, "dp", shift_x(k)) for a, k in zip(out, (1, 2, 3))]

    def join(keep, got):
        a, b, c = (g.astype(F32) * jnp.exp2(-g[0, -1].astype(F32)) for g in got)
        return (keep + a) + (b + c)

    def by_part(sums):
        n = [2 * B * len(EARLY), 2 * B * len(LATE)]
        return [jnp.concatenate([a[:, p * k : (p + 1) * k] for a, k in zip(sums, n)], axis=1) for p in range(4)]

    held = {0: grad_pre}
    z1 = [z_step(grad_pre, 1), z_step(grad_pre, -1)]
    need = need_table(slot_col, slot_count)
    xt = turn(need, x_in)
    xts = [lax.ppermute(xt, "mp", shift_y(-k)) for k in OWNERS]
    own, *bufs = pack(me, d, slot_row, slot_col, slot_count, need, weight_blocks)
    z1, xts, bufs = tie(z1, xts, bufs)

    held[-1], held[1] = z1
    z2 = [z_step(z1[0], 1), z_step(z1[1], -1)]
    bufs = [lax.ppermute(a, "mp", shift_y(-k)) for a, k in zip(bufs, OWNERS)]
    xts = [xt, *xts]
    cols = jnp.stack([a[0, : 2 * NY * NZ] for a in xts]).astype(I32)
    z2, cols = tie(z2, cols)

    held[-2], held[2] = z2
    z3 = [z_step(z2[0], 1), z_step(z2[1], -1)]
    grads = early(me, cols, xts, [held[k] for k in EARLY])
    z3, bufs, grads = tie(z3, bufs, grads)
    early_sum = lax.psum_scatter(grads, "dp", scatter_dimension=0, tiled=True)

    held[-3], held[3] = z3
    half = T // 2
    z4 = [z_step(z3[0][:half], 1), z_step(z3[1][half:], -1)]
    near = jnp.stack(bufs)
    far = core_step(near)
    accs = inputs(ROUNDS[0], me, d, cols, own, near, far, [held[k] for k in ROUNDS[0]], ())
    z4, accs = tie(z4, accs)

    held[4] = jnp.concatenate(z4, axis=0)
    mine, other = late(me, d, cols, xts, [held[k] for k in LATE])
    theirs = core_step(other)
    accs = inputs(ROUNDS[1], me, d, cols, own, near, far, [after(held[4], other)], accs)
    totals = [accs[0], *y_back(accs[1:3])]
    keep, out = pair_step(mine, theirs)
    got = x_step(out)
    totals.append(lax.ppermute(after(accs[3], got), "mp", shift_y(OWNERS[2])))
    first, *back = by_part([early_sum, join(keep, got)])
    parts = [first, *y_back(back)]
    grad_x = ((totals[0] + totals[1]) + (totals[2] + totals[3])).astype(BF16)
    return grad_x, slots(me, slot_row, slot_col, slot_count, after(need, grad_x), parts)


def solution(mesh):
    placed = (P("dp", "mp"), P("dp", "mp"), P("mp", None, None), P("mp"), P("mp"), P("mp"))
    return jax.shard_map(
        on_device,
        mesh=mesh,
        in_specs=placed,
        out_specs=(P("dp", "mp"), P("mp", "dp", None)),
        check_vma=False,
    )
```

time: 549 us -> 196 us (0.36)
  waiting for transfers between devices: 238 us -> 72.1 us
  local copies, waits for them, and re-layouts: 173 us -> 20.2 us
  matrix products: 104 us -> 0 us
  starting transfers between devices: 0.08 us -> 38.4 us
  Pallas kernels: 0 us -> 37 us
  other arithmetic: 16.2 us -> 10.1 us
    all_gather x1 -> x0, waiting for transfers between devices: 187 us -> none  [on_device(): whole = lax.all_gather(grad_pre, 'mp', axis=1, tiled=True)]
    dot_general x24 -> x0, matrix products: 104 us -> none  [the longest x8 44.8 us: advance(): total = total + jnp.einsum('tgj,gr->trj', contrib, place, precision=high)]
    gather x16 -> x0, local copies, waits for them, and re-layouts: 90.3 us -> none  [the longest x8 72.9 us: advance(): p_blocks = jnp.take(source, picks, axis=1)]
    ppermute x0 -> x25, waiting for transfers between devices: none -> 72.1 us  [the longest x5 17.1 us: y_back(): return [lax.ppermute(a, 'mp', shift_y(k)) for a, k in zip(parts, OWNERS)]]
    reduce_scatter x1, waiting for transfers between devices: 50.9 us -> 0.01 us  [on_device(): early_sum = lax.psum_scatter(grads, 'dp', scatter_dimension=0, tiled=True)]
    transpose x8 -> x0, local copies, waits for them, and re-layouts: 43.5 us -> none  [advance(): jnp.einsum('tgk,gjk->tgj', p_blocks, weights, preferred_element_type=jnp....]
    ppermute x0 -> x25, starting transfers between devices: none -> 38.4 us  [the longest x8 13.5 us: z_step(): return lax.ppermute(a, 'mp', shift_z(k))]
    pallas_call x0 -> x8, Pallas kernels: none -> 37 us  [the longest x2 13.1 us: inputs(): pl.pallas_call(lambda *refs: inputs_kernel(stage, first, *refs), out_shap...]
  transfers between devices with their start and end apart: 2 -> 26, of which waited for: 2 -> 10; matrix products, arithmetic and copies ran while one was open for 0% -> 9% of each run, Pallas kernels for 0% -> 17%
where the time goes in v1:
time: 196 us
  waiting for transfers between devices  72.1 us (37%)
  starting transfers between devices  38.4 us (20%)
  Pallas kernels  37 us (19%)
  local copies, waits for them, and re-layouts  20.2 us (10%)
  between operations  17.8 us (9%)
  other arithmetic  10.1 us (5%)
    ppermute x5, waiting for transfers between devices, y_back(): return [lax.ppermute(a, 'mp', shift_y(k)) for a, k in zip(parts, OWNERS)]  17.1 us
    ppermute x8, starting transfers between devices, z_step(): return lax.ppermute(a, 'mp', shift_z(k))  13.5 us
    pallas_call x2, Pallas kernels, inputs(): pl.pallas_call(lambda *refs: inputs_kernel(stage, first, *refs), out_shap...  13.1 us
    unnamed x51, local copies, waits for them, and re-layouts  12.1 us
    ppermute x3, waiting for transfers between devices, on_device(): bufs = [lax.ppermute(a, 'mp', shift_y(-k)) for a, k in zip(bufs, OWNERS)]  11.7 us
    ppermute x1, waiting for transfers between devices, on_device(): totals.append(lax.ppermute(after(accs[3], got), 'mp', shift_y(OWNERS[2])))  11 us
    ppermute x8, waiting for transfers between devices, z_step(): return lax.ppermute(a, 'mp', shift_z(k))  10.8 us
    ppermute x3, waiting for transfers between devices, x_step(): return [lax.ppermute(a, 'dp', shift_x(k)) for a, k in zip(out, (1, 2, 3))]  8.76 us
  transfers between devices with their start and end apart: 26, of which 10 were waited for; matrix products, arithmetic and copies ran while one was open for 9% of the time, Pallas kernels for 17%

profile of v1, /device:TPU:1, one launch (start us, length us, event | category | flops | bytes accessed | tf_op | source)
XLA Modules:
  0.0 195.6 jit_solution(14603823345973588619)
XLA Ops:
  7.2 6.5 %collective-permute-start.1 = (bf16[512,768]{1,0:T(8,128)(2,1)}, bf16[512,768]{1,0:T(8,128)(2,1)S(1)}, u32[]{:S(2)}, u32[]{:S(2)}) collective-permute-start(bf16[512,768]{1,0:T(8,128)(2,1)} %refs_6_.1), channel_id=1, source_target_pairs={{0,7},{1,0},{2,1},{3,2},{4,3},{5,4},{6,5},{7,6},{8,15},{9,8},{10,9... | collective-permute-start | bytes 2359304 | tf_op jit(solution)/shard_map/ppermute | solution.py:290
  18.4 3.0 %collective-permute-start.4 = (bf16[400,512]{1,0:T(8,128)(2,1)S(1)}, bf16[400,512]{1,0:T(8,128)(2,1)S(1)}, u32[]{:S(2)}, u32[]{:S(2)}) collective-permute-start(bf16[400,512]{1,0:T(8,128)(2,1)S(1)} %turn.1.refs_0_), channel_id=1, source_target_pairs={{0,16},{1,17},{2,18},{3,19},{4,20},{5,21},{6,22},{7,23},{8,24},{9,... | collective-permute-start | bytes 1228808 | tf_op jit(solution)/shard_map/ppermute | solution.py:321
  26.2 5.6 %pack.1 = (bf16[8,384,256]{2,1,0:T(8,128)(2,1)S(1)}, bf16[4,384,256]{2,1,0:T(8,128)(2,1)}, bf16[4,384,256]{2,1,0:T(8,128)(2,1)}, bf16[4,384,256]{2,1,0:T(8,128)(2,1)}) custom-call(s32[1]{0:T(128)} %bitcast.me.refs_0_, s32[1]{0:T(128)} %bitcast.1.d.refs_1_, s32[128]{0:T(128)S(1)} %copy-done.19, s32[128]{0:T(128)S(1)} %copy-done.17, s32[1]{0:T(128)S(6)} %copy.9.count, ...), custom_call_target="tpu_custom_call" | custom-call | bytes 7340032 | tf_op jit(solution)/shard_map/pack/pallas_call | solution.py:83
  32.9 7.4 %collective-permute-done.3.refs_2_ = bf16[400,512]{1,0:T(8,128)(2,1)} collective-permute-done((bf16[400,512]{1,0:T(8,128)(2,1)S(1)}, bf16[400,512]{1,0:T(8,128)(2,1)}, u32[]{:S(2)}, u32[]{:S(2)}) %collective-permute-start.3) | collective-permute-done | bytes 409632 | tf_op jit(solution)/shard_map/ppermute | solution.py:321
  40.4 2.7 %collective-permute-start.6 = (bf16[512,768]{1,0:T(8,128)(2,1)S(1)}, bf16[512,768]{1,0:T(8,128)(2,1)}, u32[]{:S(2)}, u32[]{:S(2)}) collective-permute-start(bf16[512,768]{1,0:T(8,128)(2,1)S(1)} %collective-permute-done.1.refs_5_.refs_7_), channel_id=1, source_target_pairs={{0,7},{1,0},{2,1},{3,2},{4,3},{5,4},{6,5},{7,6},{8,15},{9,8},{10,9... | collective-permute-start | bytes 2359304 | tf_op jit(solution)/shard_map/ppermute | solution.py:290
  45.2 2.7 %collective-permute-start.9 = (bf16[4,384,256]{2,1,0:T(8,128)(2,1)}, bf16[4,384,256]{2,1,0:T(8,128)(2,1)}, u32[]{:S(2)}, u32[]{:S(2)}) collective-permute-start(bf16[4,384,256]{2,1,0:T(8,128)(2,1)} %get-tuple-element.54), channel_id=1, source_target_pairs={{0,24},{1,25},{2,26},{3,27},{4,28},{5,29},{6,30},{7,31},{8,0},{9,1... | collective-permute-start | bytes 2359304 | tf_op jit(solution)/shard_map/ppermute | solution.py:327
  49.1 10.8 %collective-permute-done.5.refs_8_.refs_10_ = bf16[512,768]{1,0:T(8,128)(2,1)S(1)} collective-permute-done((bf16[512,768]{1,0:T(8,128)(2,1)S(1)}, bf16[512,768]{1,0:T(8,128)(2,1)S(1)}, u32[]{:S(2)}, u32[]{:S(2)}) %collective-permute-start.5) | collective-permute-done | bytes 786464 | tf_op jit(solution)/shard_map/ppermute | solution.py:290
  59.9 2.7 %collective-permute-start.8 = (bf16[512,768]{1,0:T(8,128)(2,1)}, bf16[512,768]{1,0:T(8,128)(2,1)}, u32[]{:S(2)}, u32[]{:S(2)}) collective-permute-start(bf16[512,768]{1,0:T(8,128)(2,1)} %collective-permute-done.6.refs_7_.refs_9_), channel_id=1, source_target_pairs={{0,7},{1,0},{2,1},{3,2},{4,3},{5,4},{6,5},{7,6},{8,15},{9,8},{10,9... | collective-permute-start | bytes 2359304 | tf_op jit(solution)/shard_map/ppermute | solution.py:290
  63.6 7.0 %early.1 = f32[384,5120]{1,0:T(8,128)} custom-call(s32[1]{0:T(128)} %bitcast.me.refs_0_, s32[4,64]{1,0:T(4,128)S(1)} %maximum_convert_fusion.cols.refs_2_, bf16[400,512]{1,0:T(8,128)(2,1)S(1)} %turn.1.refs_0_, bf16[400,512]{1,0:T(8,128)(2,1)} %collective-permute-done.2.refs_1_, bf16[400,512]{1,0:T(8,128)(2,1)} %collective-permute-done.3.refs_2_, ...), custom_call_target="tpu_custom_call" | custom-call | flops 2013265920 | bytes 13369344 | tf_op jit(solution)/shard_map/early/pallas_call | solution.py:115
  71.2 11.7 %collective-permute-done.11 = bf16[4,384,256]{2,1,0:T(8,128)(2,1)} collective-permute-done((bf16[4,384,256]{2,1,0:T(8,128)(2,1)}, bf16[4,384,256]{2,1,0:T(8,128)(2,1)}, u32[]{:S(2)}, u32[]{:S(2)}) %collective-permute-start.11) | collective-permute-done | bytes 786464 | tf_op jit(solution)/shard_map/ppermute | solution.py:327
  84.9 3.4 %collective-permute-start.12 = (bf16[3,4,384,256]{3,2,1,0:T(8,128)(2,1)S(1)}, bf16[3,4,384,256]{3,2,1,0:T(8,128)(2,1)S(1)}, u32[]{:S(2)}, u32[]{:S(2)}) collective-permute-start(bf16[3,4,384,256]{3,2,1,0:T(8,128)(2,1)S(1)} %pad_maximum_fusion.refs_4_), channel_id=1, source_target_pairs={{0,32},{32,0},{64,96},{96,64},{128,160},{160,128},{192,224},{224,1... | collective-permute-start | bytes 7077896 | tf_op jit(solution)/shard_map/ppermute | solution.py:293
  93.9 7.9 %inputs.2 = (f32[512,384]{1,0:T(8,128)S(1)}, f32[512,384]{1,0:T(8,128)S(1)}, f32[512,384]{1,0:T(8,128)S(1)}, f32[512,384]{1,0:T(8,128)S(1)}) custom-call(s32[1]{0:T(128)} %bitcast.me.refs_0_, s32[1]{0:T(128)} %bitcast.1.d.refs_1_, s32[4,64]{1,0:T(4,128)S(1)} %copy-done.15, bf16[8,384,256]{2,1,0:T(8,128)(2,1)} %copy-done, ...), custom_call_target="tpu_custom_call" | custom-call | flops 2818572288 | bytes 10485760 | tf_op jit(solution)/shard_map/inputs/pallas_call | solution.py:187
  104.6 5.5 %late.1 = (f32[192,3200]{1,0:T(8,128)}, f32[192,3200]{1,0:T(8,128)}) custom-call(s32[1]{0:T(128)} %bitcast.me.refs_0_, s32[1]{0:T(128)} %bitcast.1.d.refs_1_, s32[4,64]{1,0:T(4,128)S(1)} %copy-done.15, bf16[400,512]{1,0:T(8,128)(2,1)S(1)} %turn.1.refs_0_, bf16[400,512]{1,0:T(8,128)(2,1)} %collective-permute-done.2.refs_1_, ...), custom_call_target="tpu_custom_call" | custom-call | flops 1207959552 | bytes 8650752 | tf_op jit(solution)/shard_map/late/pallas_call | solution.py:152
  110.6 4.7 %collective-permute-done.17 = f32[192,3200]{1,0:T(8,128)S(1)} collective-permute-done((f32[192,3200]{1,0:T(8,128)}, f32[192,3200]{1,0:T(8,128)S(1)}, u32[]{:S(2)}, u32[]{:S(2)}) %collective-permute-start.17) | collective-permute-done | bytes 2457632 | tf_op jit(solution)/shard_map/ppermute | solution.py:293
  116.7 2.4 %fusion.1 = f32[]{:T(128)} fusion(f32[192,3200]{1,0:T(8,128)S(1)} %collective-permute-done.17, f32[192,3200]{1,0:T(8,128)} %get-tuple-element.78), kind=kLoop, calls=%fused_computation.3 | loop fusion | flops 1382399 | bytes 3686404 | tf_op jit(solution)/shard_map/reduce_max | solution.py:300
  119.9 2.4 %fusion.6 = (f16[48,3200]{1,0:T(8,128)(2,1)S(1)}, f16[48,3200]{1,0:T(8,128)(2,1)S(1)}, f16[48,3200]{1,0:T(8,128)(2,1)S(1)}) fusion(f32[192,3200]{1,0:T(8,128)} %copy-done.23, f32[192,3200]{1,0:T(8,128)} %get-tuple-element.78, f32[]{:T(128)S(6)} %floor.3, f32[]{:T(128)S(6)} %exp2.37, pred[3200]{0:T(1024)(128)(4,1)S(1)} %iota_compare_fusion), kind=kLoop, calls=%fused_computation.11 | loop fusion | flops 1843200 | bytes 4611208 | tf_op jit(solution)/shard_map/convert_element_type | solution.py:304
  122.2 2.3 %collective-permute-start.20 = (f16[48,3200]{1,0:T(8,128)(2,1)S(1)}, f16[48,3200]{1,0:T(8,128)(2,1)S(1)}, u32[]{:S(2)}, u32[]{:S(2)}) collective-permute-start(f16[48,3200]{1,0:T(8,128)(2,1)S(1)} %get-tuple-element.82), channel_id=1, source_target_pairs={{0,192},{32,224},{64,0},{96,32},{128,64},{160,96},{192,128},{224,1... | collective-permute-start | bytes 921608 | tf_op jit(solution)/shard_map/ppermute | solution.py:307
  126.2 5.2 %inputs.3 = (f32[512,384]{1,0:T(8,128)S(1)}, f32[512,384]{1,0:T(8,128)}, f32[512,384]{1,0:T(8,128)}, f32[512,384]{1,0:T(8,128)}) custom-call(s32[1]{0:T(128)} %bitcast.me.refs_0_, s32[1]{0:T(128)} %bitcast.1.d.refs_1_, s32[4,64]{1,0:T(4,128)S(1)} %copy-done.16, bf16[8,384,256]{2,1,0:T(8,128)(2,1)} %copy-done, bf16[3,4,384,256]{3,2,1,0:T(8,128)(2,1)} %copy-done.21, ...), custom_call_target="tpu_custom_call" | custom-call | flops 402653184 | bytes 10485760 | tf_op jit(solution)/shard_map/inputs/pallas_call | solution.py:187
  131.4 2.7 %collective-permute-start.16 = (f32[512,384]{1,0:T(8,128)}, f32[512,384]{1,0:T(8,128)S(1)}, u32[]{:S(2)}, u32[]{:S(2)}) collective-permute-start(f32[512,384]{1,0:T(8,128)} %get-tuple-element.76), channel_id=1, source_target_pairs={{0,24},{1,25},{2,26},{3,27},{4,28},{5,29},{6,30},{7,31},{8,0},{9,1... | collective-permute-start | bytes 2359304 | tf_op jit(solution)/shard_map/ppermute | solution.py:296
  139.6 5.9 %collective-permute-done.18 = f16[48,3200]{1,0:T(8,128)(2,1)S(1)} collective-permute-done((f16[48,3200]{1,0:T(8,128)(2,1)S(1)}, f16[48,3200]{1,0:T(8,128)(2,1)S(1)}, u32[]{:S(2)}, u32[]{:S(2)}) %collective-permute-start.18) | collective-permute-done | bytes 307232 | tf_op jit(solution)/shard_map/ppermute | solution.py:307
  152.9 2.4 %collective-permute-start.23 = (f32[48,2048]{1,0:T(8,128)S(1)}, f32[48,2048]{1,0:T(8,128)S(1)}, u32[]{:S(2)}, u32[]{:S(2)}) collective-permute-start(f32[48,2048]{1,0:T(8,128)S(1)} %pad_maximum_fusion.3), channel_id=1, source_target_pairs={{0,24},{1,25},{2,26},{3,27},{4,28},{5,29},{6,30},{7,31},{8,0},{9,1... | collective-permute-start | bytes 1179656 | tf_op jit(solution)/shard_map/ppermute | solution.py:296
  156.3 11.0 %collective-permute-done.21 = f32[512,384]{1,0:T(8,128)S(1)} collective-permute-done((f32[512,384]{1,0:T(8,128)}, f32[512,384]{1,0:T(8,128)S(1)}, u32[]{:S(2)}, u32[]{:S(2)}) %collective-permute-start.21) | collective-permute-done | bytes 786464 | tf_op jit(solution)/shard_map/ppermute | solution.py:353
  168.3 17.1 %collective-permute-done.22.refs_1_ = f32[48,2048]{1,0:T(8,128)S(1)} collective-permute-done((f32[48,2048]{1,0:T(8,128)S(1)}, f32[48,2048]{1,0:T(8,128)S(1)}, u32[]{:S(2)}, u32[]{:S(2)}) %collective-permute-start.22) | collective-permute-done | bytes 393248 | tf_op jit(solution)/shard_map/ppermute | solution.py:296
  185.4 3.4 %slots.1 = f32[128,16,128]{2,1,0:T(8,128)} custom-call(s32[1]{0:T(128)} %bitcast.me.refs_0_, s32[128]{0:T(128)S(1)} %copy-done.20, s32[128]{0:T(128)S(1)} %copy-done.18, s32[1]{0:T(128)S(6)} %copy.9.count, s32[32,128]{1,0:T(8,128)S(1)} %copy-done.13, f32[48,2048]{1,0:T(8,128)S(1)} %pad_maximum_fusion.1.refs_0_, ...), custom_call_target="tpu_custom_call" | custom-call | bytes 5242880 | tf_op jit(solution)/shard_map/slots/pallas_call | solution.py:248
  (111 shorter events, 41.4 us)
Async XLA Ops:
  7.2 142.9 %reduce-scatter.2.cloned.1.call-start = ((), (), s32[]{:S(2)}) async-start(), calls=%async_computation.1 | async-start | bytes 8847360 | tf_op jit(solution)/shard_map/reduce_scatter | solution.py:336
  7.2 33.1 %collective-permute-start.1 = (bf16[512,768]{1,0:T(8,128)(2,1)}, bf16[512,768]{1,0:T(8,128)(2,1)S(1)}, u32[]{:S(2)}, u32[]{:S(2)}) collective-permute-start(bf16[512,768]{1,0:T(8,128)(2,1)} %refs_6_.1), channel_id=1, source_target_pairs={{0,7},{1,0},{2,1},{3,2},{4,3},{5,4},{6,5},{7,6},{8,15},{9,8},{10,9... | collective-permute-start | bytes 2359304 | tf_op jit(solution)/shard_map/ppermute | solution.py:290
  13.7 26.6 %collective-permute-start = (bf16[512,768]{1,0:T(8,128)(2,1)}, bf16[512,768]{1,0:T(8,128)(2,1)S(1)}, u32[]{:S(2)}, u32[]{:S(2)}) collective-permute-start(bf16[512,768]{1,0:T(8,128)(2,1)} %refs_6_.1), channel_id=1, source_target_pairs={{0,1},{1,2},{2,3},{3,4},{4,5},{5,6},{6,7},{7,0},{8,9},{9,10},{10,1... | collective-permute-start | bytes 2359304 | tf_op jit(solution)/shard_map/ppermute | solution.py:290
  18.4 14.4 %collective-permute-start.4 = (bf16[400,512]{1,0:T(8,128)(2,1)S(1)}, bf16[400,512]{1,0:T(8,128)(2,1)S(1)}, u32[]{:S(2)}, u32[]{:S(2)}) collective-permute-start(bf16[400,512]{1,0:T(8,128)(2,1)S(1)} %turn.1.refs_0_), channel_id=1, source_target_pairs={{0,16},{1,17},{2,18},{3,19},{4,20},{5,21},{6,22},{7,23},{8,24},{9,... | collective-permute-start | bytes 1228808 | tf_op jit(solution)/shard_map/ppermute | solution.py:321
  21.5 18.9 %collective-permute-start.3 = (bf16[400,512]{1,0:T(8,128)(2,1)S(1)}, bf16[400,512]{1,0:T(8,128)(2,1)}, u32[]{:S(2)}, u32[]{:S(2)}) collective-permute-start(bf16[400,512]{1,0:T(8,128)(2,1)S(1)} %turn.1.refs_0_), channel_id=1, source_target_pairs={{0,8},{1,9},{2,10},{3,11},{4,12},{5,13},{6,14},{7,15},{8,16},{9,17... | collective-permute-start | bytes 1228808 | tf_op jit(solution)/shard_map/ppermute | solution.py:321
  21.8 18.5 %collective-permute-start.2 = (bf16[400,512]{1,0:T(8,128)(2,1)S(1)}, bf16[400,512]{1,0:T(8,128)(2,1)}, u32[]{:S(2)}, u32[]{:S(2)}) collective-permute-start(bf16[400,512]{1,0:T(8,128)(2,1)S(1)} %turn.1.refs_0_), channel_id=1, source_target_pairs={{0,24},{1,25},{2,26},{3,27},{4,28},{5,29},{6,30},{7,31},{8,0},{9,1... | collective-permute-start | bytes 1228808 | tf_op jit(solution)/shard_map/ppermute | solution.py:321
  40.3 19.6 %collective-permute-start.5 = (bf16[512,768]{1,0:T(8,128)(2,1)S(1)}, bf16[512,768]{1,0:T(8,128)(2,1)S(1)}, u32[]{:S(2)}, u32[]{:S(2)}) collective-permute-start(bf16[512,768]{1,0:T(8,128)(2,1)S(1)} %collective-permute-done.refs_6_.refs_8_), channel_id=1, source_target_pairs={{0,1},{1,2},{2,3},{3,4},{4,5},{5,6},{6,7},{7,0},{8,9},{9,10},{10,1... | collective-permute-start | bytes 2359304 | tf_op jit(solution)/shard_map/ppermute | solution.py:290
  40.4 19.5 %collective-permute-start.6 = (bf16[512,768]{1,0:T(8,128)(2,1)S(1)}, bf16[512,768]{1,0:T(8,128)(2,1)}, u32[]{:S(2)}, u32[]{:S(2)}) collective-permute-start(bf16[512,768]{1,0:T(8,128)(2,1)S(1)} %collective-permute-done.1.refs_5_.refs_7_), channel_id=1, source_target_pairs={{0,7},{1,0},{2,1},{3,2},{4,3},{5,4},{6,5},{7,6},{8,15},{9,8},{10,9... | collective-permute-start | bytes 2359304 | tf_op jit(solution)/shard_map/ppermute | solution.py:290
  45.2 26.0 %collective-permute-start.9 = (bf16[4,384,256]{2,1,0:T(8,128)(2,1)}, bf16[4,384,256]{2,1,0:T(8,128)(2,1)}, u32[]{:S(2)}, u32[]{:S(2)}) collective-permute-start(bf16[4,384,256]{2,1,0:T(8,128)(2,1)} %get-tuple-element.54), channel_id=1, source_target_pairs={{0,24},{1,25},{2,26},{3,27},{4,28},{5,29},{6,30},{7,31},{8,0},{9,1... | collective-permute-start | bytes 2359304 | tf_op jit(solution)/shard_map/ppermute | solution.py:327
  47.9 23.3 %collective-permute-start.10 = (bf16[4,384,256]{2,1,0:T(8,128)(2,1)}, bf16[4,384,256]{2,1,0:T(8,128)(2,1)}, u32[]{:S(2)}, u32[]{:S(2)}) collective-permute-start(bf16[4,384,256]{2,1,0:T(8,128)(2,1)} %get-tuple-element.55), channel_id=1, source_target_pairs={{0,8},{1,9},{2,10},{3,11},{4,12},{5,13},{6,14},{7,15},{8,16},{9,17... | collective-permute-start | bytes 2359304 | tf_op jit(solution)/shard_map/ppermute | solution.py:327
  47.9 35.0 %collective-permute-start.11 = (bf16[4,384,256]{2,1,0:T(8,128)(2,1)}, bf16[4,384,256]{2,1,0:T(8,128)(2,1)}, u32[]{:S(2)}, u32[]{:S(2)}) collective-permute-start(bf16[4,384,256]{2,1,0:T(8,128)(2,1)} %get-tuple-element.56), channel_id=1, source_target_pairs={{0,16},{1,17},{2,18},{3,19},{4,20},{5,21},{6,22},{7,23},{8,24},{9,... | collective-permute-start | bytes 2359304 | tf_op jit(solution)/shard_map/ppermute | solution.py:327
  59.9 23.0 %collective-permute-start.7 = (bf16[512,768]{1,0:T(8,128)(2,1)S(1)}, bf16[512,768]{1,0:T(8,128)(2,1)}, u32[]{:S(2)}, u32[]{:S(2)}) collective-permute-start(bf16[512,768]{1,0:T(8,128)(2,1)S(1)} %collective-permute-done.5.refs_8_.refs_10_), channel_id=1, source_target_pairs={{0,1},{1,2},{2,3},{3,4},{4,5},{5,6},{6,7},{7,0},{8,9},{9,10},{10,1... | collective-permute-start | bytes 2359304 | tf_op jit(solution)/shard_map/ppermute | solution.py:290
  59.9 23.0 %collective-permute-start.8 = (bf16[512,768]{1,0:T(8,128)(2,1)}, bf16[512,768]{1,0:T(8,128)(2,1)}, u32[]{:S(2)}, u32[]{:S(2)}) collective-permute-start(bf16[512,768]{1,0:T(8,128)(2,1)} %collective-permute-done.6.refs_7_.refs_9_), channel_id=1, source_target_pairs={{0,7},{1,0},{2,1},{3,2},{4,3},{5,4},{6,5},{7,6},{8,15},{9,8},{10,9... | collective-permute-start | bytes 2359304 | tf_op jit(solution)/shard_map/ppermute | solution.py:290
  90.3 14.2 %collective-permute-start.14 = (bf16[256,768]{1,0:T(8,128)(2,1)S(1)}, bf16[256,768]{1,0:T(8,128)(2,1)S(1)}, u32[]{:S(2)}, u32[]{:S(2)}) collective-permute-start(bf16[256,768]{1,0:T(8,128)(2,1)S(1)} %slice.86), channel_id=1, source_target_pairs={{0,7},{1,0},{2,1},{3,2},{4,3},{5,4},{6,5},{7,6},{8,15},{9,8},{10,9... | collective-permute-start | bytes 1179656 | tf_op jit(solution)/shard_map/ppermute | solution.py:290
  91.8 12.7 %collective-permute-start.13 = (bf16[256,768]{1,0:T(8,128)(2,1)S(1)}, bf16[256,768]{1,0:T(8,128)(2,1)S(1)}, u32[]{:S(2)}, u32[]{:S(2)}) collective-permute-start(bf16[256,768]{1,0:T(8,128)(2,1)S(1)} %slice.85), channel_id=1, source_target_pairs={{0,1},{1,2},{2,3},{3,4},{4,5},{5,6},{6,7},{7,0},{8,9},{9,10},{10,1... | collective-permute-start | bytes 1179656 | tf_op jit(solution)/shard_map/ppermute | solution.py:290
  122.2 12.5 %collective-permute-start.20 = (f16[48,3200]{1,0:T(8,128)(2,1)S(1)}, f16[48,3200]{1,0:T(8,128)(2,1)S(1)}, u32[]{:S(2)}, u32[]{:S(2)}) collective-permute-start(f16[48,3200]{1,0:T(8,128)(2,1)S(1)} %get-tuple-element.82), channel_id=1, source_target_pairs={{0,192},{32,224},{64,0},{96,32},{128,64},{160,96},{192,128},{224,1... | collective-permute-start | bytes 921608 | tf_op jit(solution)/shard_map/ppermute | solution.py:307
  124.6 13.6 %collective-permute-start.19 = (f16[48,3200]{1,0:T(8,128)(2,1)S(1)}, f16[48,3200]{1,0:T(8,128)(2,1)S(1)}, u32[]{:S(2)}, u32[]{:S(2)}) collective-permute-start(f16[48,3200]{1,0:T(8,128)(2,1)S(1)} %get-tuple-element.83), channel_id=1, source_target_pairs={{0,128},{32,160},{64,192},{96,224},{128,0},{160,32},{192,64},{224,... | collective-permute-start | bytes 921608 | tf_op jit(solution)/shard_map/ppermute | solution.py:307
  125.4 20.1 %collective-permute-start.18 = (f16[48,3200]{1,0:T(8,128)(2,1)S(1)}, f16[48,3200]{1,0:T(8,128)(2,1)S(1)}, u32[]{:S(2)}, u32[]{:S(2)}) collective-permute-start(f16[48,3200]{1,0:T(8,128)(2,1)S(1)} %get-tuple-element.84), channel_id=1, source_target_pairs={{0,64},{32,96},{64,128},{96,160},{128,192},{160,224},{192,0},{224,... | collective-permute-start | bytes 921608 | tf_op jit(solution)/shard_map/ppermute | solution.py:307
  131.4 23.9 %collective-permute-start.15 = (f32[512,384]{1,0:T(8,128)}, f32[512,384]{1,0:T(8,128)S(1)}, u32[]{:S(2)}, u32[]{:S(2)}) collective-permute-start(f32[512,384]{1,0:T(8,128)} %get-tuple-element.75), channel_id=1, source_target_pairs={{0,8},{1,9},{2,10},{3,11},{4,12},{5,13},{6,14},{7,15},{8,16},{9,17... | collective-permute-start | bytes 2359304 | tf_op jit(solution)/shard_map/ppermute | solution.py:296
  131.4 25.0 %collective-permute-start.16 = (f32[512,384]{1,0:T(8,128)}, f32[512,384]{1,0:T(8,128)S(1)}, u32[]{:S(2)}, u32[]{:S(2)}) collective-permute-start(f32[512,384]{1,0:T(8,128)} %get-tuple-element.76), channel_id=1, source_target_pairs={{0,24},{1,25},{2,26},{3,27},{4,28},{5,29},{6,30},{7,31},{8,0},{9,1... | collective-permute-start | bytes 2359304 | tf_op jit(solution)/shard_map/ppermute | solution.py:296
  146.9 20.5 %collective-permute-start.21 = (f32[512,384]{1,0:T(8,128)}, f32[512,384]{1,0:T(8,128)S(1)}, u32[]{:S(2)}, u32[]{:S(2)}) collective-permute-start(f32[512,384]{1,0:T(8,128)} %get-tuple-element.79), channel_id=1, source_target_pairs={{0,16},{1,17},{2,18},{3,19},{4,20},{5,21},{6,22},{7,23},{8,24},{9,... | collective-permute-start | bytes 2359304 | tf_op jit(solution)/shard_map/ppermute | solution.py:353
  152.4 33.0 %collective-permute-start.22 = (f32[48,2048]{1,0:T(8,128)S(1)}, f32[48,2048]{1,0:T(8,128)S(1)}, u32[]{:S(2)}, u32[]{:S(2)}) collective-permute-start(f32[48,2048]{1,0:T(8,128)S(1)} %pad_maximum_fusion.2), channel_id=1, source_target_pairs={{0,8},{1,9},{2,10},{3,11},{4,12},{5,13},{6,14},{7,15},{8,16},{9,17... | collective-permute-start | bytes 1179656 | tf_op jit(solution)/shard_map/ppermute | solution.py:296
  152.9 32.5 %collective-permute-start.23 = (f32[48,2048]{1,0:T(8,128)S(1)}, f32[48,2048]{1,0:T(8,128)S(1)}, u32[]{:S(2)}, u32[]{:S(2)}) collective-permute-start(f32[48,2048]{1,0:T(8,128)S(1)} %pad_maximum_fusion.3), channel_id=1, source_target_pairs={{0,24},{1,25},{2,26},{3,27},{4,28},{5,29},{6,30},{7,31},{8,0},{9,1... | collective-permute-start | bytes 1179656 | tf_op jit(solution)/shard_map/ppermute | solution.py:296
  155.3 30.0 %collective-permute-start.24 = (f32[48,2048]{1,0:T(8,128)S(1)}, f32[48,2048]{1,0:T(8,128)S(1)}, u32[]{:S(2)}, u32[]{:S(2)}) collective-permute-start(f32[48,2048]{1,0:T(8,128)S(1)} %pad_maximum_fusion.4), channel_id=1, source_target_pairs={{0,16},{1,17},{2,18},{3,19},{4,20},{5,21},{6,22},{7,23},{8,24},{9,... | collective-permute-start | bytes 1179656 | tf_op jit(solution)/shard_map/ppermute | solution.py:296
  (27 other events, 224.4 us)
Sparse Core Ops, SparseCore 0:
  83.1 63.9 reduce-scatter.1

commit v2 on v1

v2 whole, which is shorter than its diff:
```python
import math

import jax
import jax.numpy as jnp
from jax import lax
from jax.experimental import pallas as pl
from jax.experimental.pallas import tpu as pltpu
from jax.sharding import PartitionSpec as P

NY, NZ = 4, 8
NX = 4
B = 128
T = 512
CB, RB = 6, 3
D = RB * B
SLOTS = 128
EARLY, LATE = (0, 1, -1, 2, -2), (3, -3, 4)
ORDER = EARLY + LATE
ROUNDS = ((0, 1, -1, 2, -2, 3, -3), (4,))
OWNERS = (1, -1, 2)
DY_PART = (0, 2, 3, 1)
HEAD = 16

VMEM = pl.BlockSpec(memory_space=pltpu.VMEM)
SMEM = pl.BlockSpec(memory_space=pltpu.SMEM)
PARAMS = pltpu.CompilerParams(vmem_limit_bytes=48 << 20)
F32, BF16, I32 = jnp.float32, jnp.bfloat16, jnp.int32


def sds(shape, dtype):
    return jax.ShapeDtypeStruct(shape, dtype)


def cost(flops, moved):
    return pl.CostEstimate(flops=flops, bytes_accessed=moved, transcendentals=0)


def source_column(col):
    src = (col * 43691) >> 18
    return src, col - src * CB


def turn_kernel(col, count, x, need, out):
    n = NY * NZ
    shape = (SLOTS, SLOTS)
    src, c = source_column(jnp.broadcast_to(col[...], shape).T)
    lane = lax.broadcasted_iota(I32, shape, 1)
    hit = (src == (lane & (n - 1))) & (lax.broadcasted_iota(I32, shape, 0) < count[0])
    lo = jnp.min(jnp.where(hit, c, CB), axis=0, keepdims=True)
    hi = jnp.max(jnp.where(hit, c, -1), axis=0, keepdims=True)
    row = jnp.where(hi < 0, 0, jnp.where(lane[:1] < n, lo, hi))
    need[...] = jnp.broadcast_to(row, need.shape)
    out[:HEAD, :] = jnp.zeros((HEAD, T), BF16)
    out[:HEAD, :SLOTS] = jnp.broadcast_to(row, (HEAD, SLOTS)).astype(F32).astype(BF16)
    held = x[...].T
    for to in range(2 * NX):
        for r in range(RB):
            at = HEAD + (to * RB + r) * 16
            out[at : at + 16, :] = held[r * B + to * 16 : r * B + to * 16 + 16, :]


def turn(slot_col, slot_count, x):
    return pl.pallas_call(
        turn_kernel,
        out_shape=(sds((8, SLOTS), I32), sds((HEAD + D, T), BF16)),
        in_specs=[VMEM, SMEM, VMEM],
        out_specs=(VMEM, VMEM),
        compiler_params=PARAMS,
        cost_estimate=cost(0, 1 << 20),
        name="turn",
    )(slot_col.reshape(1, SLOTS), slot_count, x)


def heads_kernel(a, b, c, d, out):
    for i, head in enumerate((a, b, c, d)):
        out[i : i + 1, :] = head[...].astype(F32).astype(I32)[:1]


def heads(xts):
    return pl.pallas_call(
        heads_kernel,
        out_shape=sds((4, SLOTS), I32),
        grid=(1,),
        in_specs=[pl.BlockSpec((HEAD, SLOTS), lambda i: (0, 0))] * 4,
        out_specs=pl.BlockSpec((4, SLOTS), lambda i: (0, 0)),
        cost_estimate=cost(0, 1 << 14),
        name="heads",
    )(*xts)


def pack_kernel(me, d, row, col, count, need, w, own, b1, b2, b3, held):
    y = me[0] >> 3
    held[...] = jnp.zeros_like(held)

    @pl.loop(0, SLOTS, unroll=4)
    def _(s):
        src, c = source_column(col[s])
        p = jnp.where(c == need[0, src], 0, 1)
        at = jnp.where(s < count[0], (src - (y << 3)) & (NY * NZ - 1), NY * NZ)
        rows = pl.ds(pl.multiple_of(p * B, B), B)
        held[at, rows, pl.ds(pl.multiple_of(row[s] * B, B), B)] = w[s].T

    own[...] = held[:NZ]
    lo = (d[0] & 1) * (NZ // 2)
    for out, t in ((b1, 3), (b2, 1), (b3, 2)):
        out[...] = held[pl.ds(t * NZ + lo, NZ // 2)]


def pack(me, d, slot_row, slot_col, slot_count, need, w):
    part = sds((NZ // 2, 2 * B, D), BF16)
    return pl.pallas_call(
        pack_kernel,
        out_shape=(sds((NZ, 2 * B, D), BF16), part, part, part),
        in_specs=[SMEM] * 6 + [VMEM],
        out_specs=(VMEM,) * 4,
        scratch_shapes=[pltpu.VMEM((NY * NZ + 1, 2 * B, D), BF16)],
        compiler_params=PARAMS,
        cost_estimate=cost(0, 7 << 20),
        name="pack",
    )(me, d, slot_row, slot_col, slot_count, need, w)


def two_columns(gs, cols, part, src, sel):
    for p in range(2):
        lanes = pl.ds(pl.multiple_of(cols[part, p * NY * NZ + src] * B, B), B)
        at = 0
        for g in gs:
            sel[at : at + g.shape[0], p * B : (p + 1) * B] = g[:, lanes]
            at += g.shape[0]
    return sel[...]


def by_source(stage, refs):
    refs = list(refs)
    return [[refs.pop(0) for _ in range(2 if dz == 4 else 1)] for dz in stage]


def early_kernel(me, cols, *refs):
    xts, gs, (out, sel) = refs[:4], by_source(EARLY, refs[4:-2]), refs[-2:]
    lo = 0
    for part in range(4):
        for i, dz in enumerate(EARLY):
            src = (me[0] & ~(NZ - 1)) + ((me[0] + dz) & (NZ - 1))
            blk = two_columns(gs[i], cols, part, src, sel.at[(part * len(EARLY) + i) % 2])
            out[:, lo : lo + 2 * B] = jnp.dot(xts[part][HEAD:, :], blk, preferred_element_type=F32)
            lo += 2 * B


def early(me, cols, xts, gs):
    width = 4 * 2 * B * len(gs)
    return pl.pallas_call(
        early_kernel,
        out_shape=sds((D, width), F32),
        in_specs=[SMEM] * 2 + [VMEM] * (4 + len(gs)),
        out_specs=VMEM,
        scratch_shapes=[pltpu.VMEM((2, T, 2 * B), BF16)],
        compiler_params=PARAMS,
        cost_estimate=cost(2 * width * T * D, D * width * 4 + len(gs) * T * CB * B * 2 + 8 * T * D),
        name="early",
    )(me, cols, *xts, *gs)


def late_kernel(me, d, cols, *refs):
    xts, gs, (mine, other, turned, sel) = refs[:4], by_source(LATE, refs[4:-4]), refs[-4:]
    half, step = D // 2, RB * 16
    dx, dc = d[0] >> 1, d[0] & 1
    lo = 0
    for part in range(4):
        for cc in range(2):
            for xx in range(NX):
                to = (((dx + xx) & (NX - 1)) << 1) + (dc ^ cc)
                rows = pl.ds(pl.multiple_of(HEAD + to * step, 16), step)
                at = (cc * NX + xx) * step
                turned[at : at + step, :] = xts[part][rows, :]
        for i, dz in enumerate(LATE):
            src = (me[0] & ~(NZ - 1)) + ((me[0] + dz) & (NZ - 1))
            blk = two_columns(gs[i], cols, part, src, sel.at[(part * len(LATE) + i) % 2])
            prod = jnp.dot(turned[...], blk, preferred_element_type=F32)
            mine[:, lo : lo + 2 * B] = prod[:half]
            other[:, lo : lo + 2 * B] = prod[half:]
            lo += 2 * B


def late(me, d, cols, xts, gs):
    width = 4 * 2 * B * len(LATE)
    return pl.pallas_call(
        late_kernel,
        out_shape=(sds((D // 2, width), F32),) * 2,
        in_specs=[SMEM] * 3 + [VMEM] * (4 + len(gs)),
        out_specs=(VMEM,) * 2,
        scratch_shapes=[pltpu.VMEM((D, T), BF16), pltpu.VMEM((2, T, 2 * B), BF16)],
        compiler_params=PARAMS,
        cost_estimate=cost(2 * width * T * D, D * width * 4 + len(gs) * T * CB * B * 2 + 8 * T * D),
        name="late",
    )(me, d, cols, *xts, *gs)


def inputs_kernel(me, d, cols, own, near, far, *refs):
    gs, outs, kept, sel = by_source(ROUNDS[0], refs[:-6]), refs[-6:-2], refs[-2], refs[-1]

    def weights(part, dz):
        z = (me[0] + dz) & (NZ - 1)
        if part == 0:
            return own[z]
        at = z & (NZ // 2 - 1)
        mine = (z >> 2) == (d[0] & 1)
        return jnp.where(mine, near[part - 1, at], far[part - 1, at])

    for part in range(4):
        total = None
        for i, dz in enumerate(ROUNDS[0]):
            src = (me[0] & ~(NZ - 1)) + ((me[0] + dz) & (NZ - 1))
            blk = two_columns(gs[i], cols, part, src, sel.at[i % 2])
            prod = jnp.dot(blk, weights(part, dz), preferred_element_type=F32)
            total = prod if total is None else total + prod
        outs[part][...] = total
        for i, dz in enumerate(ROUNDS[1]):
            kept[part, i] = weights(part, dz)


def inputs(me, d, cols, own, near, far, gs):
    flops = 4 * 2 * T * D * 2 * B * len(ROUNDS[0])
    return pl.pallas_call(
        inputs_kernel,
        out_shape=(sds((T, D), F32),) * 4 + (sds((4, len(ROUNDS[1]), 2 * B, D), BF16),),
        in_specs=[SMEM] * 3 + [VMEM] * (3 + len(gs)),
        out_specs=(VMEM,) * 5,
        scratch_shapes=[pltpu.VMEM((2, T, 2 * B), BF16)],
        compiler_params=PARAMS,
        cost_estimate=cost(flops, 10 << 20),
        name="inputs",
    )(me, d, cols, own, near, far, *gs)


def rest_kernel(me, cols, kept, *refs):
    gs, accs, outs, sel = by_source(ROUNDS[1], refs[:-9]), refs[-9:-5], refs[-5:-1], refs[-1]
    for part in (1, 2, 3, 0):
        total = accs[part][...]
        for i, dz in enumerate(ROUNDS[1]):
            src = (me[0] & ~(NZ - 1)) + ((me[0] + dz) & (NZ - 1))
            blk = two_columns(gs[i], cols, part, src, sel.at[part % 2])
            total = total + jnp.dot(blk, kept[part, i], preferred_element_type=F32)
        outs[part][...] = total


def rest(me, cols, kept, gs, accs):
    flops = 4 * 2 * T * D * 2 * B * len(ROUNDS[1])
    return pl.pallas_call(
        rest_kernel,
        out_shape=(sds((T, D), F32),) * 4,
        in_specs=[SMEM] * 2 + [VMEM] * (1 + len(gs) + len(accs)),
        out_specs=(VMEM,) * 4,
        scratch_shapes=[pltpu.VMEM((2, T, 2 * B), BF16)],
        compiler_params=PARAMS,
        cost_estimate=cost(flops, 8 << 20),
        name="rest",
    )(me, cols, kept, *gs, *accs)


def scaled(out, top):
    width = out.shape[1] - B
    power = jnp.floor(14 - jnp.log(jnp.maximum(top, 1e-30)) * (1 / math.log(2)))
    out[:, :width] = out[:, :width] * jnp.exp2(power)
    out[:, width:] = jnp.broadcast_to(power, (out.shape[0], B))


def unscaled(g):
    width = g.shape[1] - B
    return g[:, :width] * jnp.exp2(-g[:1, width : width + 1])


def pair_kernel(mine, theirs, keep, *outs):
    step, width = keep.shape
    keep[...] = mine[:step, :] + theirs[:step, :]
    for i, out in enumerate(outs):
        rows = slice((i + 1) * step, (i + 2) * step)
        total = mine[rows, :] + theirs[rows, :]
        out[:, :width] = total
        scaled(out, jnp.max(jnp.abs(total), keepdims=True))


def pair(mine, theirs):
    step, width = RB * 16, mine.shape[1]
    return pl.pallas_call(
        pair_kernel,
        out_shape=(sds((step, width), F32),) + (sds((step, width + B), F32),) * 3,
        in_specs=[VMEM] * 2,
        out_specs=(VMEM,) * 4,
        compiler_params=PARAMS,
        cost_estimate=cost(0, 3 * mine.shape[0] * width * 4),
        name="pair",
    )(mine, theirs)


def join_kernel(first, keep, a, b, c, *outs):
    n = first.shape[1] // 4
    k = keep.shape[1] // 4
    total = keep[...]
    for g in (a, b, c):
        total = total + unscaled(g)
    for part, out in enumerate(outs):
        out[:, :n] = first[:, part * n : (part + 1) * n]
        out[:, n : n + k] = total[:, part * k : (part + 1) * k]
        if part > 0:
            scaled(out, jnp.max(jnp.abs(out[:, : n + k]), keepdims=True))


def join(first, keep, got):
    width = (first.shape[1] + keep.shape[1]) // 4
    return pl.pallas_call(
        join_kernel,
        out_shape=(sds((RB * 16, width), F32),) + (sds((RB * 16, width + B), F32),) * 3,
        in_specs=[VMEM] * 5,
        out_specs=(VMEM,) * 4,
        compiler_params=PARAMS,
        cost_estimate=cost(0, 4 << 20),
        name="join",
    )(first, keep, *got)


def slots_kernel(me, row, col, count, need, *refs):
    ins, out, held = refs[:-2], refs[-2], refs[-1]
    wide = 2 * B
    for part in range(4):
        sums = unscaled(ins[part]) if part > 0 else ins[part][...]
        for i, dz in enumerate(ORDER):
            held[dz & (NZ - 1), part] = sums[:, i * wide : (i + 1) * wide]
    y, z = me[0] >> 3, me[0] & 7

    @pl.loop(0, SLOTS, unroll=4)
    def _(s):
        src, c = source_column(col[s])
        p = jnp.where(c == need[0, src], 0, 1)
        dz = ((src & 7) - z) & (NZ - 1)
        dy = ((src >> 3) - y) & (NY - 1)
        part = jnp.where(dy == 0, DY_PART[0], jnp.where(dy == 1, DY_PART[1], jnp.where(dy == 2, DY_PART[2], DY_PART[3])))
        rows = pl.ds(pl.multiple_of(row[s] * 16, 16), 16)
        lanes = pl.ds(pl.multiple_of(p * B, B), B)
        blk = held[dz, part, rows, lanes]
        out[s] = jnp.where(s < count[0], blk, jnp.zeros_like(blk))


def slots(me, row, col, count, need, parts):
    return pl.pallas_call(
        slots_kernel,
        out_shape=sds((SLOTS, 16, B), F32),
        in_specs=[SMEM] * 5 + [VMEM] * len(parts),
        out_specs=VMEM,
        scratch_shapes=[pltpu.VMEM((NZ, 4, RB * 16, 2 * B), F32)],
        compiler_params=PARAMS,
        cost_estimate=cost(0, 5 << 20),
        name="slots",
    )(me, row, col, count, need, *parts)


def shift_z(k):
    return [(y * NZ + z, y * NZ + (z + k) % NZ) for y in range(NY) for z in range(NZ)]


def shift_y(k):
    return [(y * NZ + z, (y + k) % NY * NZ + z) for y in range(NY) for z in range(NZ)]


def shift_x(k):
    return [(x * 2 + c, (x + k) % NX * 2 + c) for x in range(NX) for c in range(2)]


def tie(*trees):
    return lax.optimization_barrier(trees)


def after(a, first):
    return lax.optimization_barrier((a, first))[0]


def tie(*trees):
    return lax.optimization_barrier(trees)


def on_device(x_in, grad_pre, weight_blocks, slot_row, slot_col, slot_count):
    me = lax.axis_index("mp").astype(I32).reshape(1)
    d = lax.axis_index("dp").astype(I32).reshape(1)

    def z_step(a, k):
        return lax.ppermute(a, "mp", shift_z(k))

    def core_step(a):
        return lax.ppermute(a, "dp", [(a, a ^ 1) for a in range(2 * NX)])

    def y_back(parts, owners=OWNERS):
        return [lax.ppermute(a, "mp", shift_y(k)) for a, k in zip(parts, owners)]

    def x_step(out):
        return [lax.ppermute(a, "dp", shift_x(k)) for a, k in zip(out, (1, 2, 3))]

    held = {0: grad_pre}
    z1 = [z_step(grad_pre, 1), z_step(grad_pre, -1)]
    need, xt = turn(slot_col, slot_count, x_in)
    xts = [lax.ppermute(xt, "mp", shift_y(-k)) for k in OWNERS]
    own, *bufs = pack(me, d, slot_row, slot_col, slot_count, need, weight_blocks)
    z1, xts, bufs = tie(z1, xts, bufs)

    held[-1], held[1] = z1
    z2 = [z_step(z1[0], 1), z_step(z1[1], -1)]
    bufs = [lax.ppermute(a, "mp", shift_y(-k)) for a, k in zip(bufs, OWNERS)]
    xts = [xt, *xts]
    cols = heads(xts)
    z2, cols = tie(z2, cols)

    held[-2], held[2] = z2
    z3 = [z_step(z2[0], 1), z_step(z2[1], -1)]
    grads = early(me, cols, xts, [held[k] for k in EARLY])
    z3, bufs, grads = tie(z3, bufs, grads)
    early_sum = lax.psum_scatter(grads, "dp", scatter_dimension=0, tiled=True)

    held[-3], held[3] = z3
    half = T // 2
    z4 = [z_step(z3[0][:half], 1), z_step(z3[1][half:], -1)]
    near = jnp.stack(bufs)
    far = core_step(near)
    *accs, kept = inputs(me, d, cols, own, near, far, [held[k] for k in ROUNDS[0]])
    z4, accs, kept = tie(z4, accs, kept)

    mine, other = late(me, d, cols, xts, [held[3], held[-3], *z4])
    theirs = core_step(other)
    accs = rest(me, cols, kept, z4, after(accs, other))
    totals = [accs[0], *y_back(accs[1:3])]
    keep, *out = pair(after(mine, accs), theirs)
    out = [a.astype(jnp.float16) for a in out]
    got = x_step(out)
    totals += y_back([after(accs[3], (got[2], totals[1:]))], OWNERS[2:])
    got, totals[1:3] = tie(got, totals[1:3])
    first, *back = join(early_sum, keep, [a.astype(F32) for a in got])
    parts = [first] + [a.astype(F32) for a in y_back([a.astype(jnp.float16) for a in back])]
    grad_x = ((totals[0] + totals[1]) + (totals[2] + totals[3])).astype(BF16)
    return grad_x, slots(me, slot_row, slot_col, slot_count, after(need, grad_x), parts)


def solution(mesh):
    placed = (P("dp", "mp"), P("dp", "mp"), P("mp", None, None), P("mp"), P("mp"), P("mp"))
    return jax.shard_map(
        on_device,
        mesh=mesh,
        in_specs=placed,
        out_specs=(P("dp", "mp"), P("mp", "dp", None)),
        check_vma=False,
    )
```

time: 196 us -> 174 us (0.89)
  waiting for transfers between devices: 72.1 us -> 59 us
  other arithmetic: 10.1 us -> 4.41 us
  local copies, waits for them, and re-layouts: 20.2 us -> 14.9 us
  between operations: 17.8 us -> 15 us
  Pallas kernels: 37 us -> 39.7 us
  starting transfers between devices: 38.4 us -> 40.7 us
    ppermute x6, waiting for transfers between devices: 28.1 us -> 17.7 us  [y_back(): return [lax.ppermute(a, 'mp', shift_y(k)) for a, k in zip(parts, owners)]]
    slice x9 -> x0, local copies, waits for them, and re-layouts: 6.09 us -> none  [the longest x2 2.15 us: by_part(): a[:, p * k:(p + 1) * k]]
    ppermute x3, waiting for transfers between devices: 8.76 us -> 14.4 us  [x_step(): return [lax.ppermute(a, 'dp', shift_x(k)) for a, k in zip(out, (1, 2, 3))]]
    ppermute x2, waiting for transfers between devices: 5.25 us -> 0.57 us  [core_step(): return lax.ppermute(a, 'dp', [(a, a ^ 1) for a in range(2 * NX)])]
    ppermute x3, waiting for transfers between devices: 11.7 us -> 8.53 us  [on_device(): bufs = [lax.ppermute(a, 'mp', shift_y(-k)) for a, k in zip(bufs, OWNERS)]]
    pallas_call x6 -> x8, Pallas kernels: 26.6 us -> 29.4 us  [the longest x1 8.41 us: inputs(): pl.pallas_call(inputs_kernel, out_shape=(sds((T, D), F32),) * 4 + (sds((4...]
    reduce_max x1 -> x0, other arithmetic: 2.4 us -> none  [pair_step(): top = jnp.max(jnp.abs(mine[step:] + theirs[step:]))]
    convert_element_type x2 -> x12, other arithmetic: 2.39 us -> 0.39 us  [the longest x3 0.13 us: on_device(): first, *back = join(early_sum, keep, [a.astype(F32) for a in got])]
  transfers between devices with their start and end apart: 26 -> 26, of which waited for: 10 -> 10; matrix products, arithmetic and copies ran while one was open for 9% -> 4% of each run, Pallas kernels for 17% -> 21%
where the time goes in v2:
time: 174 us
  waiting for transfers between devices  59 us (34%)
  starting transfers between devices  40.7 us (23%)
  Pallas kernels  39.7 us (23%)
  between operations  15 us (9%)
  local copies, waits for them, and re-layouts  14.9 us (9%)
  other arithmetic  4.41 us (3%)
    ppermute x6, waiting for transfers between devices, y_back(): return [lax.ppermute(a, 'mp', shift_y(k)) for a, k in zip(parts, owners)]  17.7 us
    ppermute x3, waiting for transfers between devices, x_step(): return [lax.ppermute(a, 'dp', shift_x(k)) for a, k in zip(out, (1, 2, 3))]  14.4 us
    ppermute x8, starting transfers between devices, z_step(): return lax.ppermute(a, 'mp', shift_z(k))  13.5 us
    unnamed x64, local copies, waits for them, and re-layouts  12.9 us
    ppermute x8, waiting for transfers between devices, z_step(): return lax.ppermute(a, 'mp', shift_z(k))  11.6 us
    ppermute x3, waiting for transfers between devices, on_device(): bufs = [lax.ppermute(a, 'mp', shift_y(-k)) for a, k in zip(bufs, OWNERS)]  8.53 us
    pallas_call x1, Pallas kernels, inputs(): pl.pallas_call(inputs_kernel, out_shape=(sds((T, D), F32),) * 4 + (sds((4...  8.41 us
    ppermute x6, starting transfers between devices, y_back(): return [lax.ppermute(a, 'mp', shift_y(k)) for a, k in zip(parts, owners)]  7.98 us
  transfers between devices with their start and end apart: 26, of which 10 were waited for; matrix products, arithmetic and copies ran while one was open for 4% of the time, Pallas kernels for 21%

profile of v2, /device:TPU:1, one launch (start us, length us, event | category | flops | bytes accessed | tf_op | source)
XLA Modules:
  0.0 173.7 jit_solution(13439623860637098817)
XLA Ops:
  7.2 6.5 %collective-permute-start.1 = (bf16[512,768]{1,0:T(8,128)(2,1)}, bf16[512,768]{1,0:T(8,128)(2,1)S(1)}, u32[]{:S(2)}, u32[]{:S(2)}) collective-permute-start(bf16[512,768]{1,0:T(8,128)(2,1)} %refs_0_.1), channel_id=1, source_target_pairs={{0,7},{1,0},{2,1},{3,2},{4,3},{5,4},{6,5},{7,6},{8,15},{9,8},{10,9... | collective-permute-start | bytes 2359304 | tf_op jit(solution)/shard_map/ppermute | solution.py:385
  16.2 3.0 %collective-permute-start.4 = (bf16[400,512]{1,0:T(8,128)(2,1)S(1)}, bf16[400,512]{1,0:T(8,128)(2,1)S(1)}, u32[]{:S(2)}, u32[]{:S(2)}) collective-permute-start(bf16[400,512]{1,0:T(8,128)(2,1)S(1)} %get-tuple-element.63.a.refs_0_), channel_id=1, source_target_pairs={{0,16},{1,17},{2,18},{3,19},{4,20},{5,21},{6,22},{7,23},{8,24},{9,... | collective-permute-start | bytes 1228808 | tf_op jit(solution)/shard_map/ppermute | solution.py:399
  19.6 2.3 %collective-permute-start.2 = (bf16[400,512]{1,0:T(8,128)(2,1)S(1)}, bf16[400,512]{1,0:T(8,128)(2,1)}, u32[]{:S(2)}, u32[]{:S(2)}) collective-permute-start(bf16[400,512]{1,0:T(8,128)(2,1)S(1)} %get-tuple-element.63.a.refs_0_), channel_id=1, source_target_pairs={{0,24},{1,25},{2,26},{3,27},{4,28},{5,29},{6,30},{7,31},{8,0},{9,1... | collective-permute-start | bytes 1228808 | tf_op jit(solution)/shard_map/ppermute | solution.py:399
  23.2 7.4 %pack.1 = (bf16[8,256,384]{2,1,0:T(8,128)(2,1)S(1)}, bf16[4,256,384]{2,1,0:T(8,128)(2,1)}, bf16[4,256,384]{2,1,0:T(8,128)(2,1)}, bf16[4,256,384]{2,1,0:T(8,128)(2,1)}) custom-call(s32[1]{0:T(128)} %bitcast.me, s32[1]{0:T(128)} %bitcast.2.d, s32[128]{0:T(128)S(1)} %copy-done.23, s32[128]{0:T(128)S(1)} %copy-done.21, s32[1]{0:T(128)S(6)} %copy.8.count, ...), custom_call_target="tpu_custom_call" | custom-call | bytes 7340032 | tf_op jit(solution)/shard_map/pack/pallas_call | solution.py:111
  31.8 6.3 %collective-permute-done.3.c.refs_2_ = bf16[400,512]{1,0:T(8,128)(2,1)} collective-permute-done((bf16[400,512]{1,0:T(8,128)(2,1)S(1)}, bf16[400,512]{1,0:T(8,128)(2,1)}, u32[]{:S(2)}, u32[]{:S(2)}) %collective-permute-start.3) | collective-permute-done | bytes 409632 | tf_op jit(solution)/shard_map/ppermute | solution.py:399
  38.2 2.7 %collective-permute-start.6 = (bf16[512,768]{1,0:T(8,128)(2,1)S(1)}, bf16[512,768]{1,0:T(8,128)(2,1)}, u32[]{:S(2)}, u32[]{:S(2)}) collective-permute-start(bf16[512,768]{1,0:T(8,128)(2,1)S(1)} %collective-permute-done.1.refs_5_.refs_1_), channel_id=1, source_target_pairs={{0,7},{1,0},{2,1},{3,2},{4,3},{5,4},{6,5},{7,6},{8,15},{9,8},{10,9... | collective-permute-start | bytes 2359304 | tf_op jit(solution)/shard_map/ppermute | solution.py:385
  41.0 2.7 %collective-permute-start.9 = (bf16[4,256,384]{2,1,0:T(8,128)(2,1)}, bf16[4,256,384]{2,1,0:T(8,128)(2,1)}, u32[]{:S(2)}, u32[]{:S(2)}) collective-permute-start(bf16[4,256,384]{2,1,0:T(8,128)(2,1)} %get-tuple-element.76), channel_id=1, source_target_pairs={{0,24},{1,25},{2,26},{3,27},{4,28},{5,29},{6,30},{7,31},{8,0},{9,1... | collective-permute-start | bytes 2359304 | tf_op jit(solution)/shard_map/ppermute | solution.py:405
  46.1 11.6 %collective-permute-done.5.refs_8_.refs_4_ = bf16[512,768]{1,0:T(8,128)(2,1)S(1)} collective-permute-done((bf16[512,768]{1,0:T(8,128)(2,1)S(1)}, bf16[512,768]{1,0:T(8,128)(2,1)S(1)}, u32[]{:S(2)}, u32[]{:S(2)}) %collective-permute-start.5) | collective-permute-done | bytes 786464 | tf_op jit(solution)/shard_map/ppermute | solution.py:385
  57.7 2.7 %collective-permute-start.8 = (bf16[512,768]{1,0:T(8,128)(2,1)}, bf16[512,768]{1,0:T(8,128)(2,1)}, u32[]{:S(2)}, u32[]{:S(2)}) collective-permute-start(bf16[512,768]{1,0:T(8,128)(2,1)} %collective-permute-done.6.refs_7_.refs_3_), channel_id=1, source_target_pairs={{0,7},{1,0},{2,1},{3,2},{4,3},{5,4},{6,5},{7,6},{8,15},{9,8},{10,9... | collective-permute-start | bytes 2359304 | tf_op jit(solution)/shard_map/ppermute | solution.py:385
  63.1 7.1 %early.1 = f32[384,5120]{1,0:T(8,128)} custom-call(s32[1]{0:T(128)} %bitcast.me, s32[4,128]{1,0:T(4,128)S(1)} %copy-done.16, bf16[400,512]{1,0:T(8,128)(2,1)S(1)} %copy-done.5, bf16[400,512]{1,0:T(8,128)(2,1)} %collective-permute-done.2.b.refs_1_, bf16[400,512]{1,0:T(8,128)(2,1)} %collective-permute-done.3.c.refs_2_, bf16[400,512]{1,0:T(8,128)(2,1)S(1)} %copy-done.8, ...), custom_call_target="tpu_custom_call" | custom-call | flops 2013265920 | bytes 13369344 | tf_op jit(solution)/shard_map/early/pallas_call | solution.py:151
  70.2 8.5 %collective-permute-done.11 = bf16[4,256,384]{2,1,0:T(8,128)(2,1)} collective-permute-done((bf16[4,256,384]{2,1,0:T(8,128)(2,1)}, bf16[4,256,384]{2,1,0:T(8,128)(2,1)}, u32[]{:S(2)}, u32[]{:S(2)}) %collective-permute-start.11) | collective-permute-done | bytes 786464 | tf_op jit(solution)/shard_map/ppermute | solution.py:405
  80.7 3.4 %collective-permute-start.14 = (bf16[3,4,256,384]{3,2,1,0:T(8,128)(2,1)S(1)}, bf16[3,4,256,384]{3,2,1,0:T(8,128)(2,1)S(1)}, u32[]{:S(2)}, u32[]{:S(2)}) collective-permute-start(bf16[3,4,256,384]{3,2,1,0:T(8,128)(2,1)S(1)} %pad_maximum_fusion.near), channel_id=1, source_target_pairs={{0,32},{32,0},{64,96},{96,64},{128,160},{160,128},{192,224},{224,1... | collective-permute-start | bytes 7077896 | tf_op jit(solution)/shard_map/ppermute | solution.py:388
  89.8 8.4 %inputs.1 = (f32[512,384]{1,0:T(8,128)S(1)}, f32[512,384]{1,0:T(8,128)S(1)}, f32[512,384]{1,0:T(8,128)S(1)}, f32[512,384]{1,0:T(8,128)S(1)}, bf16[4,1,256,384]{3,2,1,0:T(8,128)(2,1)S(1)}) custom-call(s32[1]{0:T(128)} %bitcast.me, s32[1]{0:T(128)} %bitcast.2.d, s32[4,128]{1,0:T(4,128)S(1)} %copy-done.17, bf16[8,256,384]{2,1,0:T(8,128)(2,1)} %copy-done.10, ...), custom_call_target="tpu_custom_call" | custom-call | flops 2818572288 | bytes 10485760 | tf_op jit(solution)/shard_map/inputs/pallas_call | solution.py:223
  100.0 5.8 %late.1 = (f32[192,3072]{1,0:T(8,128)}, f32[192,3072]{1,0:T(8,128)}) custom-call(s32[1]{0:T(128)} %bitcast.me, s32[1]{0:T(128)} %bitcast.2.d, s32[4,128]{1,0:T(4,128)S(1)} %copy-done.17, bf16[400,512]{1,0:T(8,128)(2,1)S(1)} %copy-done.6, bf16[400,512]{1,0:T(8,128)(2,1)} %collective-permute-done.2.b.refs_1_, ...), custom_call_target="tpu_custom_call" | custom-call | flops 1207959552 | bytes 9437184 | tf_op jit(solution)/shard_map/late/pallas_call | solution.py:186
  106.3 3.5 %rest.1 = (f32[512,384]{1,0:T(8,128)S(1)}, f32[512,384]{1,0:T(8,128)S(1)}, f32[512,384]{1,0:T(8,128)S(1)}, f32[512,384]{1,0:T(8,128)}) custom-call(s32[1]{0:T(128)} %bitcast.me, s32[4,128]{1,0:T(4,128)S(1)} %copy-done.17, bf16[4,1,256,384]{3,2,1,0:T(8,128)(2,1)S(1)} %get-tuple-element.90.kept, bf16[256,768]{1,0:T(8,128)(2,1)S(1)} %collective-permute-done.12.refs_6_.refs_0_, ...), custom_call_target="tpu_custom_call" | custom-call | flops 402653184 | bytes 8388608 | tf_op jit(solution)/shard_map/rest/pallas_call | solution.py:248
  109.9 2.7 %collective-permute-start.20 = (f32[512,384]{1,0:T(8,128)S(1)}, f32[512,384]{1,0:T(8,128)S(1)}, u32[]{:S(2)}, u32[]{:S(2)}) collective-permute-start(f32[512,384]{1,0:T(8,128)S(1)} %get-tuple-element.105), channel_id=1, source_target_pairs={{0,24},{1,25},{2,26},{3,27},{4,28},{5,29},{6,30},{7,31},{8,0},{9,1... | collective-permute-start | bytes 2359304 | tf_op jit(solution)/shard_map/ppermute | solution.py:391
  116.4 2.5 %collective-permute-start.18 = (f16[48,3200]{1,0:T(8,128)(2,1)S(1)}, f16[48,3200]{1,0:T(8,128)(2,1)S(1)}, u32[]{:S(2)}, u32[]{:S(2)}) collective-permute-start(f16[48,3200]{1,0:T(8,128)(2,1)S(1)} %convert_element_type.41), channel_id=1, source_target_pairs={{0,192},{32,224},{64,0},{96,32},{128,64},{160,96},{192,128},{224,1... | collective-permute-start | bytes 921608 | tf_op jit(solution)/shard_map/ppermute | solution.py:394
  118.9 11.5 %collective-permute-done.19 = f32[512,384]{1,0:T(8,128)S(1)} collective-permute-done((f32[512,384]{1,0:T(8,128)S(1)}, f32[512,384]{1,0:T(8,128)S(1)}, u32[]{:S(2)}, u32[]{:S(2)}) %collective-permute-start.19) | collective-permute-done | bytes 786464 | tf_op jit(solution)/shard_map/ppermute | solution.py:391
  131.6 2.7 %collective-permute-start.17 = (f16[48,3200]{1,0:T(8,128)(2,1)S(1)}, f16[48,3200]{1,0:T(8,128)(2,1)S(1)}, u32[]{:S(2)}, u32[]{:S(2)}) collective-permute-start(f16[48,3200]{1,0:T(8,128)(2,1)S(1)} %convert_element_type.40), channel_id=1, source_target_pairs={{0,128},{32,160},{64,192},{96,224},{128,0},{160,32},{192,64},{224,... | collective-permute-start | bytes 921608 | tf_op jit(solution)/shard_map/ppermute | solution.py:394
  134.7 6.1 %collective-permute-done.17 = f16[48,3200]{1,0:T(8,128)(2,1)S(1)} collective-permute-done((f16[48,3200]{1,0:T(8,128)(2,1)S(1)}, f16[48,3200]{1,0:T(8,128)(2,1)S(1)}, u32[]{:S(2)}, u32[]{:S(2)}) %collective-permute-start.17) | collective-permute-done | bytes 307232 | tf_op jit(solution)/shard_map/ppermute | solution.py:394
  140.8 8.3 %collective-permute-done.16 = f16[48,3200]{1,0:T(8,128)(2,1)S(1)} collective-permute-done((f16[48,3200]{1,0:T(8,128)(2,1)S(1)}, f16[48,3200]{1,0:T(8,128)(2,1)S(1)}, u32[]{:S(2)}, u32[]{:S(2)}) %collective-permute-start.16) | collective-permute-done | bytes 307232 | tf_op jit(solution)/shard_map/ppermute | solution.py:394
  151.1 2.4 %collective-permute-start.24 = (f16[48,2176]{1,0:T(8,128)(2,1)S(1)}, f16[48,2176]{1,0:T(8,128)(2,1)S(1)}, u32[]{:S(2)}, u32[]{:S(2)}) collective-permute-start(f16[48,2176]{1,0:T(8,128)(2,1)S(1)} %convert_element_type.50), channel_id=1, source_target_pairs={{0,16},{1,17},{2,18},{3,19},{4,20},{5,21},{6,22},{7,23},{8,24},{9,... | collective-permute-start | bytes 626696 | tf_op jit(solution)/shard_map/ppermute | solution.py:391
  159.0 4.2 %collective-permute-done.23 = f16[48,2176]{1,0:T(8,128)(2,1)S(1)} collective-permute-done((f16[48,2176]{1,0:T(8,128)(2,1)S(1)}, f16[48,2176]{1,0:T(8,128)(2,1)S(1)}, u32[]{:S(2)}, u32[]{:S(2)}) %collective-permute-start.23) | collective-permute-done | bytes 208928 | tf_op jit(solution)/shard_map/ppermute | solution.py:391
  163.6 3.2 %slots.1 = f32[128,16,128]{2,1,0:T(8,128)} custom-call(s32[1]{0:T(128)} %bitcast.me, s32[128]{0:T(128)S(1)} %copy-done.24, s32[128]{0:T(128)S(1)} %copy-done.22, s32[1]{0:T(128)S(6)} %copy.8.count, s32[8,128]{1,0:T(8,128)S(1)} %copy-done.19, f32[48,2048]{1,0:T(8,128)S(1)} %get-tuple-element.120.refs_0_, f32[48,2176]{1,0:T(8,128)S(1)} %convert_element_type.47.refs_1_, ...), custom_call_target="tpu_custom_call" | custom-call | bytes 5242880 | tf_op jit(solution)/shard_map/slots/pallas_call | solution.py:344
  (119 shorter events, 33.1 us)
Async XLA Ops:
  7.2 142.1 %reduce-scatter.2.cloned.1.call-start = ((), (), s32[]{:S(2)}) async-start(), calls=%async_computation.1 | async-start | bytes 8847360 | tf_op jit(solution)/shard_map/reduce_scatter | solution.py:414
  7.2 30.9 %collective-permute-start.1 = (bf16[512,768]{1,0:T(8,128)(2,1)}, bf16[512,768]{1,0:T(8,128)(2,1)S(1)}, u32[]{:S(2)}, u32[]{:S(2)}) collective-permute-start(bf16[512,768]{1,0:T(8,128)(2,1)} %refs_0_.1), channel_id=1, source_target_pairs={{0,7},{1,0},{2,1},{3,2},{4,3},{5,4},{6,5},{7,6},{8,15},{9,8},{10,9... | collective-permute-start | bytes 2359304 | tf_op jit(solution)/shard_map/ppermute | solution.py:385
  13.7 24.4 %collective-permute-start = (bf16[512,768]{1,0:T(8,128)(2,1)}, bf16[512,768]{1,0:T(8,128)(2,1)S(1)}, u32[]{:S(2)}, u32[]{:S(2)}) collective-permute-start(bf16[512,768]{1,0:T(8,128)(2,1)} %refs_0_.1), channel_id=1, source_target_pairs={{0,1},{1,2},{2,3},{3,4},{4,5},{5,6},{6,7},{7,0},{8,9},{9,10},{10,1... | collective-permute-start | bytes 2359304 | tf_op jit(solution)/shard_map/ppermute | solution.py:385
  16.2 15.6 %collective-permute-start.4 = (bf16[400,512]{1,0:T(8,128)(2,1)S(1)}, bf16[400,512]{1,0:T(8,128)(2,1)S(1)}, u32[]{:S(2)}, u32[]{:S(2)}) collective-permute-start(bf16[400,512]{1,0:T(8,128)(2,1)S(1)} %get-tuple-element.63.a.refs_0_), channel_id=1, source_target_pairs={{0,16},{1,17},{2,18},{3,19},{4,20},{5,21},{6,22},{7,23},{8,24},{9,... | collective-permute-start | bytes 1228808 | tf_op jit(solution)/shard_map/ppermute | solution.py:399
  19.2 18.9 %collective-permute-start.3 = (bf16[400,512]{1,0:T(8,128)(2,1)S(1)}, bf16[400,512]{1,0:T(8,128)(2,1)}, u32[]{:S(2)}, u32[]{:S(2)}) collective-permute-start(bf16[400,512]{1,0:T(8,128)(2,1)S(1)} %get-tuple-element.63.a.refs_0_), channel_id=1, source_target_pairs={{0,8},{1,9},{2,10},{3,11},{4,12},{5,13},{6,14},{7,15},{8,16},{9,17... | collective-permute-start | bytes 1228808 | tf_op jit(solution)/shard_map/ppermute | solution.py:399
  19.6 18.5 %collective-permute-start.2 = (bf16[400,512]{1,0:T(8,128)(2,1)S(1)}, bf16[400,512]{1,0:T(8,128)(2,1)}, u32[]{:S(2)}, u32[]{:S(2)}) collective-permute-start(bf16[400,512]{1,0:T(8,128)(2,1)S(1)} %get-tuple-element.63.a.refs_0_), channel_id=1, source_target_pairs={{0,24},{1,25},{2,26},{3,27},{4,28},{5,29},{6,30},{7,31},{8,0},{9,1... | collective-permute-start | bytes 1228808 | tf_op jit(solution)/shard_map/ppermute | solution.py:399
  38.1 19.6 %collective-permute-start.5 = (bf16[512,768]{1,0:T(8,128)(2,1)S(1)}, bf16[512,768]{1,0:T(8,128)(2,1)S(1)}, u32[]{:S(2)}, u32[]{:S(2)}) collective-permute-start(bf16[512,768]{1,0:T(8,128)(2,1)S(1)} %collective-permute-done.refs_6_.refs_2_), channel_id=1, source_target_pairs={{0,1},{1,2},{2,3},{3,4},{4,5},{5,6},{6,7},{7,0},{8,9},{9,10},{10,1... | collective-permute-start | bytes 2359304 | tf_op jit(solution)/shard_map/ppermute | solution.py:385
  38.2 19.5 %collective-permute-start.6 = (bf16[512,768]{1,0:T(8,128)(2,1)S(1)}, bf16[512,768]{1,0:T(8,128)(2,1)}, u32[]{:S(2)}, u32[]{:S(2)}) collective-permute-start(bf16[512,768]{1,0:T(8,128)(2,1)S(1)} %collective-permute-done.1.refs_5_.refs_1_), channel_id=1, source_target_pairs={{0,7},{1,0},{2,1},{3,2},{4,3},{5,4},{6,5},{7,6},{8,15},{9,8},{10,9... | collective-permute-start | bytes 2359304 | tf_op jit(solution)/shard_map/ppermute | solution.py:385
  41.0 29.2 %collective-permute-start.9 = (bf16[4,256,384]{2,1,0:T(8,128)(2,1)}, bf16[4,256,384]{2,1,0:T(8,128)(2,1)}, u32[]{:S(2)}, u32[]{:S(2)}) collective-permute-start(bf16[4,256,384]{2,1,0:T(8,128)(2,1)} %get-tuple-element.76), channel_id=1, source_target_pairs={{0,24},{1,25},{2,26},{3,27},{4,28},{5,29},{6,30},{7,31},{8,0},{9,1... | collective-permute-start | bytes 2359304 | tf_op jit(solution)/shard_map/ppermute | solution.py:405
  43.7 26.5 %collective-permute-start.10 = (bf16[4,256,384]{2,1,0:T(8,128)(2,1)}, bf16[4,256,384]{2,1,0:T(8,128)(2,1)}, u32[]{:S(2)}, u32[]{:S(2)}) collective-permute-start(bf16[4,256,384]{2,1,0:T(8,128)(2,1)} %get-tuple-element.77), channel_id=1, source_target_pairs={{0,8},{1,9},{2,10},{3,11},{4,12},{5,13},{6,14},{7,15},{8,16},{9,17... | collective-permute-start | bytes 2359304 | tf_op jit(solution)/shard_map/ppermute | solution.py:405
  43.7 35.0 %collective-permute-start.11 = (bf16[4,256,384]{2,1,0:T(8,128)(2,1)}, bf16[4,256,384]{2,1,0:T(8,128)(2,1)}, u32[]{:S(2)}, u32[]{:S(2)}) collective-permute-start(bf16[4,256,384]{2,1,0:T(8,128)(2,1)} %get-tuple-element.78), channel_id=1, source_target_pairs={{0,16},{1,17},{2,18},{3,19},{4,20},{5,21},{6,22},{7,23},{8,24},{9,... | collective-permute-start | bytes 2359304 | tf_op jit(solution)/shard_map/ppermute | solution.py:405
  57.7 21.0 %collective-permute-start.7 = (bf16[512,768]{1,0:T(8,128)(2,1)S(1)}, bf16[512,768]{1,0:T(8,128)(2,1)}, u32[]{:S(2)}, u32[]{:S(2)}) collective-permute-start(bf16[512,768]{1,0:T(8,128)(2,1)S(1)} %collective-permute-done.5.refs_8_.refs_4_), channel_id=1, source_target_pairs={{0,1},{1,2},{2,3},{3,4},{4,5},{5,6},{6,7},{7,0},{8,9},{9,10},{10,1... | collective-permute-start | bytes 2359304 | tf_op jit(solution)/shard_map/ppermute | solution.py:385
  57.7 21.0 %collective-permute-start.8 = (bf16[512,768]{1,0:T(8,128)(2,1)}, bf16[512,768]{1,0:T(8,128)(2,1)}, u32[]{:S(2)}, u32[]{:S(2)}) collective-permute-start(bf16[512,768]{1,0:T(8,128)(2,1)} %collective-permute-done.6.refs_7_.refs_3_), channel_id=1, source_target_pairs={{0,7},{1,0},{2,1},{3,2},{4,3},{5,4},{6,5},{7,6},{8,15},{9,8},{10,9... | collective-permute-start | bytes 2359304 | tf_op jit(solution)/shard_map/ppermute | solution.py:385
  86.1 13.8 %collective-permute-start.13 = (bf16[256,768]{1,0:T(8,128)(2,1)S(1)}, bf16[256,768]{1,0:T(8,128)(2,1)S(1)}, u32[]{:S(2)}, u32[]{:S(2)}) collective-permute-start(bf16[256,768]{1,0:T(8,128)(2,1)S(1)} %slice.7), channel_id=1, source_target_pairs={{0,7},{1,0},{2,1},{3,2},{4,3},{5,4},{6,5},{7,6},{8,15},{9,8},{10,9... | collective-permute-start | bytes 1179656 | tf_op jit(solution)/shard_map/ppermute | solution.py:385
  87.6 12.4 %collective-permute-start.12 = (bf16[256,768]{1,0:T(8,128)(2,1)S(1)}, bf16[256,768]{1,0:T(8,128)(2,1)S(1)}, u32[]{:S(2)}, u32[]{:S(2)}) collective-permute-start(bf16[256,768]{1,0:T(8,128)(2,1)S(1)} %slice.6), channel_id=1, source_target_pairs={{0,1},{1,2},{2,3},{3,4},{4,5},{5,6},{6,7},{7,0},{8,9},{9,10},{10,1... | collective-permute-start | bytes 1179656 | tf_op jit(solution)/shard_map/ppermute | solution.py:385
  109.9 20.5 %collective-permute-start.19 = (f32[512,384]{1,0:T(8,128)S(1)}, f32[512,384]{1,0:T(8,128)S(1)}, u32[]{:S(2)}, u32[]{:S(2)}) collective-permute-start(f32[512,384]{1,0:T(8,128)S(1)} %get-tuple-element.104), channel_id=1, source_target_pairs={{0,8},{1,9},{2,10},{3,11},{4,12},{5,13},{6,14},{7,15},{8,16},{9,17... | collective-permute-start | bytes 2359304 | tf_op jit(solution)/shard_map/ppermute | solution.py:391
  109.9 20.5 %collective-permute-start.20 = (f32[512,384]{1,0:T(8,128)S(1)}, f32[512,384]{1,0:T(8,128)S(1)}, u32[]{:S(2)}, u32[]{:S(2)}) collective-permute-start(f32[512,384]{1,0:T(8,128)S(1)} %get-tuple-element.105), channel_id=1, source_target_pairs={{0,24},{1,25},{2,26},{3,27},{4,28},{5,29},{6,30},{7,31},{8,0},{9,1... | collective-permute-start | bytes 2359304 | tf_op jit(solution)/shard_map/ppermute | solution.py:391
  116.4 14.0 %collective-permute-start.18 = (f16[48,3200]{1,0:T(8,128)(2,1)S(1)}, f16[48,3200]{1,0:T(8,128)(2,1)S(1)}, u32[]{:S(2)}, u32[]{:S(2)}) collective-permute-start(f16[48,3200]{1,0:T(8,128)(2,1)S(1)} %convert_element_type.41), channel_id=1, source_target_pairs={{0,192},{32,224},{64,0},{96,32},{128,64},{160,96},{192,128},{224,1... | collective-permute-start | bytes 921608 | tf_op jit(solution)/shard_map/ppermute | solution.py:394
  130.4 24.9 %collective-permute-start.21 = (f32[512,384]{1,0:T(8,128)}, f32[512,384]{1,0:T(8,128)}, u32[]{:S(2)}, u32[]{:S(2)}) collective-permute-start(f32[512,384]{1,0:T(8,128)} %get-tuple-element.113), channel_id=1, source_target_pairs={{0,16},{1,17},{2,18},{3,19},{4,20},{5,21},{6,22},{7,23},{8,24},{9,... | collective-permute-start | bytes 2359304 | tf_op jit(solution)/shard_map/ppermute | solution.py:391
  131.6 9.2 %collective-permute-start.17 = (f16[48,3200]{1,0:T(8,128)(2,1)S(1)}, f16[48,3200]{1,0:T(8,128)(2,1)S(1)}, u32[]{:S(2)}, u32[]{:S(2)}) collective-permute-start(f16[48,3200]{1,0:T(8,128)(2,1)S(1)} %convert_element_type.40), channel_id=1, source_target_pairs={{0,128},{32,160},{64,192},{96,224},{128,0},{160,32},{192,64},{224,... | collective-permute-start | bytes 921608 | tf_op jit(solution)/shard_map/ppermute | solution.py:394
  134.3 14.7 %collective-permute-start.16 = (f16[48,3200]{1,0:T(8,128)(2,1)S(1)}, f16[48,3200]{1,0:T(8,128)(2,1)S(1)}, u32[]{:S(2)}, u32[]{:S(2)}) collective-permute-start(f16[48,3200]{1,0:T(8,128)(2,1)S(1)} %convert_element_type.39), channel_id=1, source_target_pairs={{0,64},{32,96},{64,128},{96,160},{128,192},{160,224},{192,0},{224,... | collective-permute-start | bytes 921608 | tf_op jit(solution)/shard_map/ppermute | solution.py:394
  151.1 7.9 %collective-permute-start.24 = (f16[48,2176]{1,0:T(8,128)(2,1)S(1)}, f16[48,2176]{1,0:T(8,128)(2,1)S(1)}, u32[]{:S(2)}, u32[]{:S(2)}) collective-permute-start(f16[48,2176]{1,0:T(8,128)(2,1)S(1)} %convert_element_type.50), channel_id=1, source_target_pairs={{0,16},{1,17},{2,18},{3,19},{4,20},{5,21},{6,22},{7,23},{8,24},{9,... | collective-permute-start | bytes 626696 | tf_op jit(solution)/shard_map/ppermute | solution.py:391
  153.5 9.8 %collective-permute-start.23 = (f16[48,2176]{1,0:T(8,128)(2,1)S(1)}, f16[48,2176]{1,0:T(8,128)(2,1)S(1)}, u32[]{:S(2)}, u32[]{:S(2)}) collective-permute-start(f16[48,2176]{1,0:T(8,128)(2,1)S(1)} %convert_element_type.48), channel_id=1, source_target_pairs={{0,24},{1,25},{2,26},{3,27},{4,28},{5,29},{6,30},{7,31},{8,0},{9,1... | collective-permute-start | bytes 626696 | tf_op jit(solution)/shard_map/ppermute | solution.py:391
  155.2 8.3 %collective-permute-start.22 = (f16[48,2176]{1,0:T(8,128)(2,1)S(1)}, f16[48,2176]{1,0:T(8,128)(2,1)S(1)}, u32[]{:S(2)}, u32[]{:S(2)}) collective-permute-start(f16[48,2176]{1,0:T(8,128)(2,1)S(1)} %convert_element_type.46), channel_id=1, source_target_pairs={{0,8},{1,9},{2,10},{3,11},{4,12},{5,13},{6,14},{7,15},{8,16},{9,17... | collective-permute-start | bytes 626696 | tf_op jit(solution)/shard_map/ppermute | solution.py:391
  (34 other events, 303.6 us)
Sparse Core Ops, SparseCore 0:
  78.8 57.4 reduce-scatter.1

commit v3 on v2

--- a/solution.py
+++ b/solution.py
@@ -233,28 +233,52 @@
 
 
 def rest_kernel(me, cols, kept, *refs):
-    gs, accs, outs, sel = by_source(ROUNDS[1], refs[:-9]), refs[-9:-5], refs[-5:-1], refs[-1]
-    for part in (1, 2, 3, 0):
+    gs, accs, outs, sel = by_source(ROUNDS[1], refs[:-10]), refs[-10:-6], refs[-6:-1], refs[-1]
+    for part in (3, 1, 2, 0):
         total = accs[part][...]
         for i, dz in enumerate(ROUNDS[1]):
             src = (me[0] & ~(NZ - 1)) + ((me[0] + dz) & (NZ - 1))
             blk = two_columns(gs[i], cols, part, src, sel.at[part % 2])
             total = total + jnp.dot(blk, kept[part, i], preferred_element_type=F32)
-        outs[part][...] = total
+        if part < 3:
+            outs[part][...] = total
+        else:
+            outs[3][...] = total[: T // 2]
+            outs[4][...] = total[T // 2 :]
 
 
 def rest(me, cols, kept, gs, accs):
     flops = 4 * 2 * T * D * 2 * B * len(ROUNDS[1])
     return pl.pallas_call(
         rest_kernel,
-        out_shape=(sds((T, D), F32),) * 4,
+        out_shape=(sds((T, D), F32),) * 3 + (sds((T // 2, D), F32),) * 2,
         in_specs=[SMEM] * 2 + [VMEM] * (1 + len(gs) + len(accs)),
-        out_specs=(VMEM,) * 4,
+        out_specs=(VMEM,) * 5,
         scratch_shapes=[pltpu.VMEM((2, T, 2 * B), BF16)],
         compiler_params=PARAMS,
         cost_estimate=cost(flops, 8 << 20),
         name="rest",
     )(me, cols, kept, *gs, *accs)
+
+
+def relay_kernel(up, down, lo, hi, up_out, down_out):
+    n = T // 2
+    up_out[:n, :] = up[:n, :] + lo[...]
+    up_out[n:, :] = up[n:, :]
+    down_out[:n, :] = down[:n, :]
+    down_out[n:, :] = down[n:, :] + hi[...]
+
+
+def relay(up, down, lo, hi):
+    return pl.pallas_call(
+        relay_kernel,
+        out_shape=(sds((T, D), F32),) * 2,
+        in_specs=[VMEM] * 4,
+        out_specs=(VMEM,) * 2,
+        compiler_params=PARAMS,
+        cost_estimate=cost(0, 5 << 20),
+        name="relay",
+    )(up, down, lo, hi)
 
 
 def scaled(out, top):
@@ -387,8 +411,8 @@
     def core_step(a):
         return lax.ppermute(a, "dp", [(a, a ^ 1) for a in range(2 * NX)])
 
-    def y_back(parts, owners=OWNERS):
-        return [lax.ppermute(a, "mp", shift_y(k)) for a, k in zip(parts, owners)]
+    def y_back(parts):
+        return [lax.ppermute(a, "mp", shift_y(k)) for a, k in zip(parts, OWNERS)]
 
     def x_step(out):
         return [lax.ppermute(a, "dp", shift_x(k)) for a, k in zip(out, (1, 2, 3))]
@@ -421,18 +445,18 @@
     *accs, kept = inputs(me, d, cols, own, near, far, [held[k] for k in ROUNDS[0]])
     z4, accs, kept = tie(z4, accs, kept)
 
-    mine, other = late(me, d, cols, xts, [held[3], held[-3], *z4])
+    total, up, down, lo, hi = rest(me, cols, kept, z4, accs)
+    lo, hi = lax.ppermute(lo, "mp", shift_y(1)), lax.ppermute(hi, "mp", shift_y(-1))
+    mine, other = late(me, d, cols, xts, after([held[3], held[-3], *z4], total))
     theirs = core_step(other)
-    accs = rest(me, cols, kept, z4, after(accs, other))
-    totals = [accs[0], *y_back(accs[1:3])]
-    keep, *out = pair(after(mine, accs), theirs)
+    keep, *out = pair(mine, theirs)
     out = [a.astype(jnp.float16) for a in out]
     got = x_step(out)
-    totals += y_back([after(accs[3], (got[2], totals[1:]))], OWNERS[2:])
-    got, totals[1:3] = tie(got, totals[1:3])
+    up, down = relay(*after((up, down), out), lo, hi)
+    up, down = lax.ppermute(up, "mp", shift_y(1)), lax.ppermute(down, "mp", shift_y(-1))
     first, *back = join(early_sum, keep, [a.astype(F32) for a in got])
     parts = [first] + [a.astype(F32) for a in y_back([a.astype(jnp.float16) for a in back])]
-    grad_x = ((totals[0] + totals[1]) + (totals[2] + totals[3])).astype(BF16)
+    grad_x = (total + (up + down)).astype(BF16)
     return grad_x, slots(me, slot_row, slot_col, slot_count, after(need, grad_x), parts)
 
 

time: 174 us -> 171 us (0.983)
  waiting for transfers between devices: 59 us -> 55.1 us
  local copies, waits for them, and re-layouts: 14.9 us -> 17.6 us
  starting transfers between devices: 40.7 us -> 38.3 us
    ppermute x6 -> x7, waiting for transfers between devices: 17.7 us -> 10.5 us  [the longest x3 8.39 us: y_back(): return [lax.ppermute(a, 'mp', shift_y(k)) for a, k in zip(parts, OWNERS)]]
    unnamed x64 -> x56, local copies, waits for them, and re-layouts: 12.9 us -> 15.5 us
    ppermute x3, starting transfers between devices: 5.62 us -> 3.33 us  [x_step(): return [lax.ppermute(a, 'dp', shift_x(k)) for a, k in zip(out, (1, 2, 3))]]
    pallas_call x1 -> x2, Pallas kernels: 3.52 us -> 3.9 us  [the longest x1 2.54 us: rest(): pl.pallas_call(rest_kernel, out_shape=(sds((T, D), F32),) * 3 + (sds((T /...]
    ppermute x6 -> x7, starting transfers between devices: 7.98 us -> 7.77 us  [the longest x1 2.67 us: on_device(): lax.ppermute(hi, 'mp', shift_y(-1))]
  transfers between devices with their start and end apart: 26 -> 27, of which waited for: 10 -> 12; matrix products, arithmetic and copies ran while one was open for 4% -> 4% of each run, Pallas kernels for 21% -> 21%
where the time goes in v3:
time: 171 us; the launch traced here: 170 us
  waiting for transfers between devices  55.1 us (32%)
  Pallas kernels  39.6 us (23%)
  starting transfers between devices  38.3 us (22%)
  local copies, waits for them, and re-layouts  17.6 us (10%)
  between operations  15 us (9%)
  other arithmetic  4.59 us (3%)
    ppermute x3, waiting for transfers between devices, x_step(): return [lax.ppermute(a, 'dp', shift_x(k)) for a, k in zip(out, (1, 2, 3))]  15.9 us
    unnamed x56, local copies, waits for them, and re-layouts  15.5 us
    ppermute x8, starting transfers between devices, z_step(): return lax.ppermute(a, 'mp', shift_z(k))  13.5 us
    ppermute x8, waiting for transfers between devices, z_step(): return lax.ppermute(a, 'mp', shift_z(k))  11.5 us
    ppermute x3, waiting for transfers between devices, on_device(): bufs = [lax.ppermute(a, 'mp', shift_y(-k)) for a, k in zip(bufs, OWNERS)]  8.56 us
    ppermute x3, waiting for transfers between devices, y_back(): return [lax.ppermute(a, 'mp', shift_y(k)) for a, k in zip(parts, OWNERS)]  8.39 us
    pallas_call x1, Pallas kernels, inputs(): pl.pallas_call(inputs_kernel, out_shape=(sds((T, D), F32),) * 4 + (sds((4...  8.31 us
    pallas_call x1, Pallas kernels, pack(): pl.pallas_call(pack_kernel, out_shape=(sds((NZ, 2 * B, D), BF16), part, p...  7.45 us
  transfers between devices with their start and end apart: 27, of which 12 were waited for; matrix products, arithmetic and copies ran while one was open for 4% of the time, Pallas kernels for 21%

profile of v3, /device:TPU:1, one launch (start us, length us, event | category | flops | bytes accessed | tf_op | source)
XLA Modules:
  0.0 170.2 jit_solution(3891470101849728937)
XLA Ops:
  7.2 6.5 %collective-permute-start.1 = (bf16[512,768]{1,0:T(8,128)(2,1)}, bf16[512,768]{1,0:T(8,128)(2,1)S(1)}, u32[]{:S(2)}, u32[]{:S(2)}) collective-permute-start(bf16[512,768]{1,0:T(8,128)(2,1)} %refs_0_.1), channel_id=1, source_target_pairs={{0,7},{1,0},{2,1},{3,2},{4,3},{5,4},{6,5},{7,6},{8,15},{9,8},{10,9... | collective-permute-start | bytes 2359304 | tf_op jit(solution)/shard_map/ppermute | solution.py:409
  16.2 3.0 %collective-permute-start.4 = (bf16[400,512]{1,0:T(8,128)(2,1)S(1)}, bf16[400,512]{1,0:T(8,128)(2,1)S(1)}, u32[]{:S(2)}, u32[]{:S(2)}) collective-permute-start(bf16[400,512]{1,0:T(8,128)(2,1)S(1)} %get-tuple-element.61.a.refs_0_), channel_id=1, source_target_pairs={{0,16},{1,17},{2,18},{3,19},{4,20},{5,21},{6,22},{7,23},{8,24},{9,... | collective-permute-start | bytes 1228808 | tf_op jit(solution)/shard_map/ppermute | solution.py:423
  19.6 2.3 %collective-permute-start.2 = (bf16[400,512]{1,0:T(8,128)(2,1)S(1)}, bf16[400,512]{1,0:T(8,128)(2,1)}, u32[]{:S(2)}, u32[]{:S(2)}) collective-permute-start(bf16[400,512]{1,0:T(8,128)(2,1)S(1)} %get-tuple-element.61.a.refs_0_), channel_id=1, source_target_pairs={{0,24},{1,25},{2,26},{3,27},{4,28},{5,29},{6,30},{7,31},{8,0},{9,1... | collective-permute-start | bytes 1228808 | tf_op jit(solution)/shard_map/ppermute | solution.py:423
  23.2 7.5 %pack.1 = (bf16[8,256,384]{2,1,0:T(8,128)(2,1)S(1)}, bf16[4,256,384]{2,1,0:T(8,128)(2,1)}, bf16[4,256,384]{2,1,0:T(8,128)(2,1)}, bf16[4,256,384]{2,1,0:T(8,128)(2,1)}) custom-call(s32[1]{0:T(128)} %bitcast.me, s32[1]{0:T(128)} %bitcast.2.d, s32[128]{0:T(128)S(1)} %copy-done.23, s32[128]{0:T(128)S(1)} %copy-done.21, s32[1]{0:T(128)S(6)} %copy.8.count, ...), custom_call_target="tpu_custom_call" | custom-call | bytes 7340032 | tf_op jit(solution)/shard_map/pack/pallas_call | solution.py:111
  31.8 6.3 %collective-permute-done.3.c.refs_2_ = bf16[400,512]{1,0:T(8,128)(2,1)} collective-permute-done((bf16[400,512]{1,0:T(8,128)(2,1)S(1)}, bf16[400,512]{1,0:T(8,128)(2,1)}, u32[]{:S(2)}, u32[]{:S(2)}) %collective-permute-start.3) | collective-permute-done | bytes 409632 | tf_op jit(solution)/shard_map/ppermute | solution.py:423
  38.2 2.7 %collective-permute-start.6 = (bf16[512,768]{1,0:T(8,128)(2,1)S(1)}, bf16[512,768]{1,0:T(8,128)(2,1)}, u32[]{:S(2)}, u32[]{:S(2)}) collective-permute-start(bf16[512,768]{1,0:T(8,128)(2,1)S(1)} %collective-permute-done.1.refs_5_.refs_1_), channel_id=1, source_target_pairs={{0,7},{1,0},{2,1},{3,2},{4,3},{5,4},{6,5},{7,6},{8,15},{9,8},{10,9... | collective-permute-start | bytes 2359304 | tf_op jit(solution)/shard_map/ppermute | solution.py:409
  41.0 2.7 %collective-permute-start.9 = (bf16[4,256,384]{2,1,0:T(8,128)(2,1)}, bf16[4,256,384]{2,1,0:T(8,128)(2,1)}, u32[]{:S(2)}, u32[]{:S(2)}) collective-permute-start(bf16[4,256,384]{2,1,0:T(8,128)(2,1)} %get-tuple-element.74), channel_id=1, source_target_pairs={{0,24},{1,25},{2,26},{3,27},{4,28},{5,29},{6,30},{7,31},{8,0},{9,1... | collective-permute-start | bytes 2359304 | tf_op jit(solution)/shard_map/ppermute | solution.py:429
  46.2 11.5 %collective-permute-done.5.refs_8_.refs_4_ = bf16[512,768]{1,0:T(8,128)(2,1)S(1)} collective-permute-done((bf16[512,768]{1,0:T(8,128)(2,1)S(1)}, bf16[512,768]{1,0:T(8,128)(2,1)S(1)}, u32[]{:S(2)}, u32[]{:S(2)}) %collective-permute-start.5) | collective-permute-done | bytes 786464 | tf_op jit(solution)/shard_map/ppermute | solution.py:409
  57.7 2.7 %collective-permute-start.8 = (bf16[512,768]{1,0:T(8,128)(2,1)}, bf16[512,768]{1,0:T(8,128)(2,1)}, u32[]{:S(2)}, u32[]{:S(2)}) collective-permute-start(bf16[512,768]{1,0:T(8,128)(2,1)} %collective-permute-done.6.refs_7_.refs_3_), channel_id=1, source_target_pairs={{0,7},{1,0},{2,1},{3,2},{4,3},{5,4},{6,5},{7,6},{8,15},{9,8},{10,9... | collective-permute-start | bytes 2359304 | tf_op jit(solution)/shard_map/ppermute | solution.py:409
  63.1 7.0 %early.1 = f32[384,5120]{1,0:T(8,128)} custom-call(s32[1]{0:T(128)} %bitcast.me, s32[4,128]{1,0:T(4,128)S(1)} %copy-done.16, bf16[400,512]{1,0:T(8,128)(2,1)S(1)} %copy-done.5, bf16[400,512]{1,0:T(8,128)(2,1)} %collective-permute-done.2.b.refs_1_, bf16[400,512]{1,0:T(8,128)(2,1)} %collective-permute-done.3.c.refs_2_, bf16[400,512]{1,0:T(8,128)(2,1)S(1)} %copy-done.8, ...), custom_call_target="tpu_custom_call" | custom-call | flops 2013265920 | bytes 13369344 | tf_op jit(solution)/shard_map/early/pallas_call | solution.py:151
  70.1 8.6 %collective-permute-done.11 = bf16[4,256,384]{2,1,0:T(8,128)(2,1)} collective-permute-done((bf16[4,256,384]{2,1,0:T(8,128)(2,1)}, bf16[4,256,384]{2,1,0:T(8,128)(2,1)}, u32[]{:S(2)}, u32[]{:S(2)}) %collective-permute-start.11) | collective-permute-done | bytes 786464 | tf_op jit(solution)/shard_map/ppermute | solution.py:429
  80.7 3.4 %collective-permute-start.14 = (bf16[3,4,256,384]{3,2,1,0:T(8,128)(2,1)S(1)}, bf16[3,4,256,384]{3,2,1,0:T(8,128)(2,1)S(1)}, u32[]{:S(2)}, u32[]{:S(2)}) collective-permute-start(bf16[3,4,256,384]{3,2,1,0:T(8,128)(2,1)S(1)} %pad_maximum_fusion.near), channel_id=1, source_target_pairs={{0,32},{32,0},{64,96},{96,64},{128,160},{160,128},{192,224},{224,1... | collective-permute-start | bytes 7077896 | tf_op jit(solution)/shard_map/ppermute | solution.py:412
  89.8 8.3 %inputs.1 = (f32[512,384]{1,0:T(8,128)S(1)}, f32[512,384]{1,0:T(8,128)S(1)}, f32[512,384]{1,0:T(8,128)S(1)}, f32[512,384]{1,0:T(8,128)S(1)}, bf16[4,1,256,384]{3,2,1,0:T(8,128)(2,1)S(1)}) custom-call(s32[1]{0:T(128)} %bitcast.me, s32[1]{0:T(128)} %bitcast.2.d, s32[4,128]{1,0:T(4,128)S(1)} %copy-done.17, bf16[8,256,384]{2,1,0:T(8,128)(2,1)} %copy-done.10, ...), custom_call_target="tpu_custom_call" | custom-call | flops 2818572288 | bytes 10485760 | tf_op jit(solution)/shard_map/inputs/pallas_call | solution.py:223
  100.9 2.5 %rest.1 = (f32[512,384]{1,0:T(8,128)S(1)}, f32[512,384]{1,0:T(8,128)S(1)}, f32[512,384]{1,0:T(8,128)S(1)}, f32[256,384]{1,0:T(8,128)S(1)}, f32[256,384]{1,0:T(8,128)S(1)}) custom-call(s32[1]{0:T(128)} %bitcast.me, s32[4,128]{1,0:T(4,128)S(1)} %copy-done.17, bf16[4,1,256,384]{3,2,1,0:T(8,128)(2,1)S(1)} %get-tuple-element.88.kept, ...), custom_call_target="tpu_custom_call" | custom-call | flops 402653184 | bytes 8388608 | tf_op jit(solution)/shard_map/rest/pallas_call | solution.py:252
  103.4 5.6 %late.1 = (f32[192,3072]{1,0:T(8,128)}, f32[192,3072]{1,0:T(8,128)}) custom-call(s32[1]{0:T(128)} %bitcast.me, s32[1]{0:T(128)} %bitcast.2.d, s32[4,128]{1,0:T(4,128)S(1)} %copy-done.17, bf16[400,512]{1,0:T(8,128)(2,1)S(1)} %copy-done.6, bf16[400,512]{1,0:T(8,128)(2,1)} %collective-permute-done.2.b.refs_1_, ...), custom_call_target="tpu_custom_call" | custom-call | flops 1207959552 | bytes 9437184 | tf_op jit(solution)/shard_map/late/pallas_call | solution.py:186
  109.6 2.7 %collective-permute-start.17 = (f32[256,384]{1,0:T(8,128)S(1)}, f32[256,384]{1,0:T(8,128)S(1)}, u32[]{:S(2)}, u32[]{:S(2)}) collective-permute-start(f32[256,384]{1,0:T(8,128)S(1)} %get-tuple-element.110), channel_id=1, source_target_pairs={{0,24},{1,25},{2,26},{3,27},{4,28},{5,29},{6,30},{7,31},{8,0},{9,1... | collective-permute-start | bytes 1179656 | tf_op jit(solution)/shard_map/ppermute | solution.py:449
  123.0 2.7 %collective-permute-start.19 = (f32[512,384]{1,0:T(8,128)}, f32[512,384]{1,0:T(8,128)}, u32[]{:S(2)}, u32[]{:S(2)}) collective-permute-start(f32[512,384]{1,0:T(8,128)} %get-tuple-element.112), channel_id=1, source_target_pairs={{0,24},{1,25},{2,26},{3,27},{4,28},{5,29},{6,30},{7,31},{8,0},{9,1... | collective-permute-start | bytes 2359304 | tf_op jit(solution)/shard_map/ppermute | solution.py:456
  129.0 4.8 %collective-permute-done.22 = f16[48,3200]{1,0:T(8,128)(2,1)S(1)} collective-permute-done((f16[48,3200]{1,0:T(8,128)(2,1)S(1)}, f16[48,3200]{1,0:T(8,128)(2,1)S(1)}, u32[]{:S(2)}, u32[]{:S(2)}) %collective-permute-start.22) | collective-permute-done | bytes 307232 | tf_op jit(solution)/shard_map/ppermute | solution.py:418
  133.9 2.4 %collective-permute-done.21 = f16[48,3200]{1,0:T(8,128)(2,1)S(1)} collective-permute-done((f16[48,3200]{1,0:T(8,128)(2,1)S(1)}, f16[48,3200]{1,0:T(8,128)(2,1)S(1)}, u32[]{:S(2)}, u32[]{:S(2)}) %collective-permute-start.21) | collective-permute-done | bytes 307232 | tf_op jit(solution)/shard_map/ppermute | solution.py:418
  136.4 8.7 %collective-permute-done.20 = f16[48,3200]{1,0:T(8,128)(2,1)S(1)} collective-permute-done((f16[48,3200]{1,0:T(8,128)(2,1)S(1)}, f16[48,3200]{1,0:T(8,128)(2,1)S(1)}, u32[]{:S(2)}, u32[]{:S(2)}) %collective-permute-start.20) | collective-permute-done | bytes 307232 | tf_op jit(solution)/shard_map/ppermute | solution.py:418
  149.3 2.3 %add_convert_fusion = bf16[512,384]{1,0:T(8,128)(2,1)} fusion(f32[512,384]{1,0:T(8,128)S(1)} %get-tuple-element.95, f32[512,384]{1,0:T(8,128)} %collective-permute-done.18, f32[512,384]{1,0:T(8,128)} %collective-permute-done.19), kind=kLoop, calls=%fused_computation.1 | loop fusion | flops 589824 | bytes 2752512 | tf_op jit(solution)/shard_map/convert_element_type | solution.py:459
  151.6 3.2 %collective-permute-done.25 = f16[48,2176]{1,0:T(8,128)(2,1)S(1)} collective-permute-done((f16[48,2176]{1,0:T(8,128)(2,1)S(1)}, f16[48,2176]{1,0:T(8,128)(2,1)S(1)}, u32[]{:S(2)}, u32[]{:S(2)}) %collective-permute-start.25) | collective-permute-done | bytes 208928 | tf_op jit(solution)/shard_map/ppermute | solution.py:415
  154.8 3.4 %collective-permute-done.24 = f16[48,2176]{1,0:T(8,128)(2,1)S(1)} collective-permute-done((f16[48,2176]{1,0:T(8,128)(2,1)S(1)}, f16[48,2176]{1,0:T(8,128)(2,1)S(1)}, u32[]{:S(2)}, u32[]{:S(2)}) %collective-permute-start.24) | collective-permute-done | bytes 208928 | tf_op jit(solution)/shard_map/ppermute | solution.py:415
  160.1 3.2 %slots.1 = f32[128,16,128]{2,1,0:T(8,128)} custom-call(s32[1]{0:T(128)} %bitcast.me, s32[128]{0:T(128)S(1)} %copy-done.24, s32[128]{0:T(128)S(1)} %copy-done.22, s32[1]{0:T(128)S(6)} %copy.8.count, s32[8,128]{1,0:T(8,128)S(1)} %copy-done.19, f32[48,2048]{1,0:T(8,128)S(1)} %get-tuple-element.116.refs_0_, f32[48,2176]{1,0:T(8,128)S(1)} %convert_element_type.47.refs_1_, ...), custom_call_target="tpu_custom_call" | custom-call | bytes 5242880 | tf_op jit(solution)/shard_map/slots/pallas_call | solution.py:368
  (114 shorter events, 41.3 us)
Async XLA Ops:
  7.2 137.9 %reduce-scatter.2.cloned.1.call-start = ((), (), s32[]{:S(2)}) async-start(), calls=%async_computation.1 | async-start | bytes 8847360 | tf_op jit(solution)/shard_map/reduce_scatter | solution.py:438
  7.2 30.9 %collective-permute-start.1 = (bf16[512,768]{1,0:T(8,128)(2,1)}, bf16[512,768]{1,0:T(8,128)(2,1)S(1)}, u32[]{:S(2)}, u32[]{:S(2)}) collective-permute-start(bf16[512,768]{1,0:T(8,128)(2,1)} %refs_0_.1), channel_id=1, source_target_pairs={{0,7},{1,0},{2,1},{3,2},{4,3},{5,4},{6,5},{7,6},{8,15},{9,8},{10,9... | collective-permute-start | bytes 2359304 | tf_op jit(solution)/shard_map/ppermute | solution.py:409
  13.7 24.4 %collective-permute-start = (bf16[512,768]{1,0:T(8,128)(2,1)}, bf16[512,768]{1,0:T(8,128)(2,1)S(1)}, u32[]{:S(2)}, u32[]{:S(2)}) collective-permute-start(bf16[512,768]{1,0:T(8,128)(2,1)} %refs_0_.1), channel_id=1, source_target_pairs={{0,1},{1,2},{2,3},{3,4},{4,5},{5,6},{6,7},{7,0},{8,9},{9,10},{10,1... | collective-permute-start | bytes 2359304 | tf_op jit(solution)/shard_map/ppermute | solution.py:409
  16.2 15.6 %collective-permute-start.4 = (bf16[400,512]{1,0:T(8,128)(2,1)S(1)}, bf16[400,512]{1,0:T(8,128)(2,1)S(1)}, u32[]{:S(2)}, u32[]{:S(2)}) collective-permute-start(bf16[400,512]{1,0:T(8,128)(2,1)S(1)} %get-tuple-element.61.a.refs_0_), channel_id=1, source_target_pairs={{0,16},{1,17},{2,18},{3,19},{4,20},{5,21},{6,22},{7,23},{8,24},{9,... | collective-permute-start | bytes 1228808 | tf_op jit(solution)/shard_map/ppermute | solution.py:423
  19.2 18.9 %collective-permute-start.3 = (bf16[400,512]{1,0:T(8,128)(2,1)S(1)}, bf16[400,512]{1,0:T(8,128)(2,1)}, u32[]{:S(2)}, u32[]{:S(2)}) collective-permute-start(bf16[400,512]{1,0:T(8,128)(2,1)S(1)} %get-tuple-element.61.a.refs_0_), channel_id=1, source_target_pairs={{0,8},{1,9},{2,10},{3,11},{4,12},{5,13},{6,14},{7,15},{8,16},{9,17... | collective-permute-start | bytes 1228808 | tf_op jit(solution)/shard_map/ppermute | solution.py:423
  19.6 18.5 %collective-permute-start.2 = (bf16[400,512]{1,0:T(8,128)(2,1)S(1)}, bf16[400,512]{1,0:T(8,128)(2,1)}, u32[]{:S(2)}, u32[]{:S(2)}) collective-permute-start(bf16[400,512]{1,0:T(8,128)(2,1)S(1)} %get-tuple-element.61.a.refs_0_), channel_id=1, source_target_pairs={{0,24},{1,25},{2,26},{3,27},{4,28},{5,29},{6,30},{7,31},{8,0},{9,1... | collective-permute-start | bytes 1228808 | tf_op jit(solution)/shard_map/ppermute | solution.py:423
  38.1 19.6 %collective-permute-start.5 = (bf16[512,768]{1,0:T(8,128)(2,1)S(1)}, bf16[512,768]{1,0:T(8,128)(2,1)S(1)}, u32[]{:S(2)}, u32[]{:S(2)}) collective-permute-start(bf16[512,768]{1,0:T(8,128)(2,1)S(1)} %collective-permute-done.refs_6_.refs_2_), channel_id=1, source_target_pairs={{0,1},{1,2},{2,3},{3,4},{4,5},{5,6},{6,7},{7,0},{8,9},{9,10},{10,1... | collective-permute-start | bytes 2359304 | tf_op jit(solution)/shard_map/ppermute | solution.py:409
  38.2 19.5 %collective-permute-start.6 = (bf16[512,768]{1,0:T(8,128)(2,1)S(1)}, bf16[512,768]{1,0:T(8,128)(2,1)}, u32[]{:S(2)}, u32[]{:S(2)}) collective-permute-start(bf16[512,768]{1,0:T(8,128)(2,1)S(1)} %collective-permute-done.1.refs_5_.refs_1_), channel_id=1, source_target_pairs={{0,7},{1,0},{2,1},{3,2},{4,3},{5,4},{6,5},{7,6},{8,15},{9,8},{10,9... | collective-permute-start | bytes 2359304 | tf_op jit(solution)/shard_map/ppermute | solution.py:409
  41.0 29.2 %collective-permute-start.9 = (bf16[4,256,384]{2,1,0:T(8,128)(2,1)}, bf16[4,256,384]{2,1,0:T(8,128)(2,1)}, u32[]{:S(2)}, u32[]{:S(2)}) collective-permute-start(bf16[4,256,384]{2,1,0:T(8,128)(2,1)} %get-tuple-element.74), channel_id=1, source_target_pairs={{0,24},{1,25},{2,26},{3,27},{4,28},{5,29},{6,30},{7,31},{8,0},{9,1... | collective-permute-start | bytes 2359304 | tf_op jit(solution)/shard_map/ppermute | solution.py:429
  43.7 26.4 %collective-permute-start.10 = (bf16[4,256,384]{2,1,0:T(8,128)(2,1)}, bf16[4,256,384]{2,1,0:T(8,128)(2,1)}, u32[]{:S(2)}, u32[]{:S(2)}) collective-permute-start(bf16[4,256,384]{2,1,0:T(8,128)(2,1)} %get-tuple-element.75), channel_id=1, source_target_pairs={{0,8},{1,9},{2,10},{3,11},{4,12},{5,13},{6,14},{7,15},{8,16},{9,17... | collective-permute-start | bytes 2359304 | tf_op jit(solution)/shard_map/ppermute | solution.py:429
  43.7 35.0 %collective-permute-start.11 = (bf16[4,256,384]{2,1,0:T(8,128)(2,1)}, bf16[4,256,384]{2,1,0:T(8,128)(2,1)}, u32[]{:S(2)}, u32[]{:S(2)}) collective-permute-start(bf16[4,256,384]{2,1,0:T(8,128)(2,1)} %get-tuple-element.76), channel_id=1, source_target_pairs={{0,16},{1,17},{2,18},{3,19},{4,20},{5,21},{6,22},{7,23},{8,24},{9,... | collective-permute-start | bytes 2359304 | tf_op jit(solution)/shard_map/ppermute | solution.py:429
  57.7 21.0 %collective-permute-start.7 = (bf16[512,768]{1,0:T(8,128)(2,1)S(1)}, bf16[512,768]{1,0:T(8,128)(2,1)}, u32[]{:S(2)}, u32[]{:S(2)}) collective-permute-start(bf16[512,768]{1,0:T(8,128)(2,1)S(1)} %collective-permute-done.5.refs_8_.refs_4_), channel_id=1, source_target_pairs={{0,1},{1,2},{2,3},{3,4},{4,5},{5,6},{6,7},{7,0},{8,9},{9,10},{10,1... | collective-permute-start | bytes 2359304 | tf_op jit(solution)/shard_map/ppermute | solution.py:409
  57.7 21.0 %collective-permute-start.8 = (bf16[512,768]{1,0:T(8,128)(2,1)}, bf16[512,768]{1,0:T(8,128)(2,1)}, u32[]{:S(2)}, u32[]{:S(2)}) collective-permute-start(bf16[512,768]{1,0:T(8,128)(2,1)} %collective-permute-done.6.refs_7_.refs_3_), channel_id=1, source_target_pairs={{0,7},{1,0},{2,1},{3,2},{4,3},{5,4},{6,5},{7,6},{8,15},{9,8},{10,9... | collective-permute-start | bytes 2359304 | tf_op jit(solution)/shard_map/ppermute | solution.py:409
  86.1 14.7 %collective-permute-start.13 = (bf16[256,768]{1,0:T(8,128)(2,1)S(1)}, bf16[256,768]{1,0:T(8,128)(2,1)S(1)}, u32[]{:S(2)}, u32[]{:S(2)}) collective-permute-start(bf16[256,768]{1,0:T(8,128)(2,1)S(1)} %slice.7), channel_id=1, source_target_pairs={{0,7},{1,0},{2,1},{3,2},{4,3},{5,4},{6,5},{7,6},{8,15},{9,8},{10,9... | collective-permute-start | bytes 1179656 | tf_op jit(solution)/shard_map/ppermute | solution.py:409
  87.6 13.3 %collective-permute-start.12 = (bf16[256,768]{1,0:T(8,128)(2,1)S(1)}, bf16[256,768]{1,0:T(8,128)(2,1)S(1)}, u32[]{:S(2)}, u32[]{:S(2)}) collective-permute-start(bf16[256,768]{1,0:T(8,128)(2,1)S(1)} %slice.6), channel_id=1, source_target_pairs={{0,1},{1,2},{2,3},{3,4},{4,5},{5,6},{6,7},{7,0},{8,9},{9,10},{10,1... | collective-permute-start | bytes 1179656 | tf_op jit(solution)/shard_map/ppermute | solution.py:409
  109.6 12.1 %collective-permute-start.16 = (f32[256,384]{1,0:T(8,128)S(1)}, f32[256,384]{1,0:T(8,128)S(1)}, u32[]{:S(2)}, u32[]{:S(2)}) collective-permute-start(f32[256,384]{1,0:T(8,128)S(1)} %get-tuple-element.109), channel_id=1, source_target_pairs={{0,8},{1,9},{2,10},{3,11},{4,12},{5,13},{6,14},{7,15},{8,16},{9,17... | collective-permute-start | bytes 1179656 | tf_op jit(solution)/shard_map/ppermute | solution.py:449
  109.6 12.1 %collective-permute-start.17 = (f32[256,384]{1,0:T(8,128)S(1)}, f32[256,384]{1,0:T(8,128)S(1)}, u32[]{:S(2)}, u32[]{:S(2)}) collective-permute-start(f32[256,384]{1,0:T(8,128)S(1)} %get-tuple-element.110), channel_id=1, source_target_pairs={{0,24},{1,25},{2,26},{3,27},{4,28},{5,29},{6,30},{7,31},{8,0},{9,1... | collective-permute-start | bytes 1179656 | tf_op jit(solution)/shard_map/ppermute | solution.py:449
  123.0 26.3 %collective-permute-start.18 = (f32[512,384]{1,0:T(8,128)}, f32[512,384]{1,0:T(8,128)}, u32[]{:S(2)}, u32[]{:S(2)}) collective-permute-start(f32[512,384]{1,0:T(8,128)} %get-tuple-element.111), channel_id=1, source_target_pairs={{0,8},{1,9},{2,10},{3,11},{4,12},{5,13},{6,14},{7,15},{8,16},{9,17... | collective-permute-start | bytes 2359304 | tf_op jit(solution)/shard_map/ppermute | solution.py:456
  123.0 26.3 %collective-permute-start.19 = (f32[512,384]{1,0:T(8,128)}, f32[512,384]{1,0:T(8,128)}, u32[]{:S(2)}, u32[]{:S(2)}) collective-permute-start(f32[512,384]{1,0:T(8,128)} %get-tuple-element.112), channel_id=1, source_target_pairs={{0,24},{1,25},{2,26},{3,27},{4,28},{5,29},{6,30},{7,31},{8,0},{9,1... | collective-permute-start | bytes 2359304 | tf_op jit(solution)/shard_map/ppermute | solution.py:456
  125.7 8.1 %collective-permute-start.22 = (f16[48,3200]{1,0:T(8,128)(2,1)S(1)}, f16[48,3200]{1,0:T(8,128)(2,1)S(1)}, u32[]{:S(2)}, u32[]{:S(2)}) collective-permute-start(f16[48,3200]{1,0:T(8,128)(2,1)S(1)} %convert_element_type.41), channel_id=1, source_target_pairs={{0,192},{32,224},{64,0},{96,32},{128,64},{160,96},{192,128},{224,1... | collective-permute-start | bytes 921608 | tf_op jit(solution)/shard_map/ppermute | solution.py:418
  127.8 8.5 %collective-permute-start.21 = (f16[48,3200]{1,0:T(8,128)(2,1)S(1)}, f16[48,3200]{1,0:T(8,128)(2,1)S(1)}, u32[]{:S(2)}, u32[]{:S(2)}) collective-permute-start(f16[48,3200]{1,0:T(8,128)(2,1)S(1)} %convert_element_type.40), channel_id=1, source_target_pairs={{0,128},{32,160},{64,192},{96,224},{128,0},{160,32},{192,64},{224,... | collective-permute-start | bytes 921608 | tf_op jit(solution)/shard_map/ppermute | solution.py:418
  128.4 16.6 %collective-permute-start.20 = (f16[48,3200]{1,0:T(8,128)(2,1)S(1)}, f16[48,3200]{1,0:T(8,128)(2,1)S(1)}, u32[]{:S(2)}, u32[]{:S(2)}) collective-permute-start(f16[48,3200]{1,0:T(8,128)(2,1)S(1)} %convert_element_type.39), channel_id=1, source_target_pairs={{0,64},{32,96},{64,128},{96,160},{128,192},{160,224},{192,0},{224,... | collective-permute-start | bytes 921608 | tf_op jit(solution)/shard_map/ppermute | solution.py:418
  147.9 10.4 %collective-permute-start.24 = (f16[48,2176]{1,0:T(8,128)(2,1)S(1)}, f16[48,2176]{1,0:T(8,128)(2,1)S(1)}, u32[]{:S(2)}, u32[]{:S(2)}) collective-permute-start(f16[48,2176]{1,0:T(8,128)(2,1)S(1)} %convert_element_type.48), channel_id=1, source_target_pairs={{0,24},{1,25},{2,26},{3,27},{4,28},{5,29},{6,30},{7,31},{8,0},{9,1... | collective-permute-start | bytes 626696 | tf_op jit(solution)/shard_map/ppermute | solution.py:415
  148.4 11.7 %collective-permute-start.23 = (f16[48,2176]{1,0:T(8,128)(2,1)S(1)}, f16[48,2176]{1,0:T(8,128)(2,1)S(1)}, u32[]{:S(2)}, u32[]{:S(2)}) collective-permute-start(f16[48,2176]{1,0:T(8,128)(2,1)S(1)} %convert_element_type.46), channel_id=1, source_target_pairs={{0,8},{1,9},{2,10},{3,11},{4,12},{5,13},{6,14},{7,15},{8,16},{9,17... | collective-permute-start | bytes 626696 | tf_op jit(solution)/shard_map/ppermute | solution.py:415
  (31 other events, 237.9 us)
Sparse Core Ops, SparseCore 0:
  78.8 51.2 reduce-scatter.1

commit v4 on v3

--- a/solution.py
+++ b/solution.py
@@ -23,7 +23,7 @@
 
 VMEM = pl.BlockSpec(memory_space=pltpu.VMEM)
 SMEM = pl.BlockSpec(memory_space=pltpu.SMEM)
-PARAMS = pltpu.CompilerParams(vmem_limit_bytes=48 << 20)
+PARAMS = pltpu.CompilerParams(vmem_limit_bytes=28 << 20)
 F32, BF16, I32 = jnp.float32, jnp.bfloat16, jnp.int32
 
 
@@ -92,7 +92,7 @@
     y = me[0] >> 3
     held[...] = jnp.zeros_like(held)
 
-    @pl.loop(0, SLOTS, unroll=4)
+    @pl.loop(0, SLOTS, unroll=8)
     def _(s):
         src, c = source_column(col[s])
         p = jnp.where(c == need[0, src], 0, 1)
@@ -351,7 +351,7 @@
             held[dz & (NZ - 1), part] = sums[:, i * wide : (i + 1) * wide]
     y, z = me[0] >> 3, me[0] & 7
 
-    @pl.loop(0, SLOTS, unroll=4)
+    @pl.loop(0, SLOTS, unroll=8)
     def _(s):
         src, c = source_column(col[s])
         p = jnp.where(c == need[0, src], 0, 1)

time: 171 us -> 168 us (0.982)
  Pallas kernels: 39.6 us -> 26.9 us
  waiting for transfers between devices: 55.1 us -> 63.2 us
  starting transfers between devices: 38.3 us -> 40.9 us
  local copies, waits for them, and re-layouts: 17.6 us -> 15.4 us
    ppermute x1, waiting for transfers between devices: 2.11 us -> 6.82 us  [on_device(): lax.ppermute(lo, 'mp', shift_y(1))]
    ppermute x8, waiting for transfers between devices: 11.5 us -> 16.1 us  [z_step(): return lax.ppermute(a, 'mp', shift_z(k))]
    pallas_call x1, Pallas kernels: 7.03 us -> 3.94 us  [early(): pl.pallas_call(early_kernel, out_shape=sds((D, width), F32), in_specs=[SM...]
    ppermute x3, waiting for transfers between devices: 8.39 us -> 5.5 us  [y_back(): return [lax.ppermute(a, 'mp', shift_y(k)) for a, k in zip(parts, OWNERS)]]
    pallas_call x1, Pallas kernels: 7.45 us -> 4.8 us  [pack(): pl.pallas_call(pack_kernel, out_shape=(sds((NZ, 2 * B, D), BF16), part, p...]
    pallas_call x1, Pallas kernels: 5.56 us -> 3.33 us  [late(): pl.pallas_call(late_kernel, out_shape=(sds((D // 2, width), F32),) * 2, i...]
    unnamed x56 -> x44, local copies, waits for them, and re-layouts: 15.5 us -> 13.3 us
    ppermute x3, starting transfers between devices: 2.42 us -> 4.31 us  [y_back(): return [lax.ppermute(a, 'mp', shift_y(k)) for a, k in zip(parts, OWNERS)]]
  transfers between devices with their start and end apart: 27 -> 27, of which waited for: 12 -> 14; matrix products, arithmetic and copies ran while one was open for 4% -> 4% of each run, Pallas kernels for 21% -> 14%
where the time goes in v4:
time: 168 us; the launch traced here: 166 us
  waiting for transfers between devices  63.2 us (38%)
  starting transfers between devices  40.9 us (24%)
  Pallas kernels  26.9 us (16%)
  local copies, waits for them, and re-layouts  15.4 us (9%)
  between operations  15 us (9%)
  other arithmetic  4.7 us (3%)
    ppermute x3, waiting for transfers between devices, x_step(): return [lax.ppermute(a, 'dp', shift_x(k)) for a, k in zip(out, (1, 2, 3))]  17.1 us
    ppermute x8, waiting for transfers between devices, z_step(): return lax.ppermute(a, 'mp', shift_z(k))  16.1 us
    ppermute x8, starting transfers between devices, z_step(): return lax.ppermute(a, 'mp', shift_z(k))  13.5 us
    unnamed x44, local copies, waits for them, and re-layouts  13.3 us
    ppermute x3, waiting for transfers between devices, on_device(): bufs = [lax.ppermute(a, 'mp', shift_y(-k)) for a, k in zip(bufs, OWNERS)]  8.57 us
    ppermute x1, waiting for transfers between devices, on_device(): lax.ppermute(lo, 'mp', shift_y(1))  6.82 us
    ppermute x3, waiting for transfers between devices, on_device(): xts = [lax.ppermute(xt, 'mp', shift_y(-k)) for k in OWNERS]  6.69 us
    pallas_call x1, Pallas kernels, inputs(): pl.pallas_call(inputs_kernel, out_shape=(sds((T, D), F32),) * 4 + (sds((4...  6.49 us
  transfers between devices with their start and end apart: 27, of which 14 were waited for; matrix products, arithmetic and copies ran while one was open for 4% of the time, Pallas kernels for 14%

profile of v4, /device:TPU:1, one launch (start us, length us, event | category | flops | bytes accessed | tf_op | source)
XLA Modules:
  0.0 166.1 jit_solution(7435950755532293313)
XLA Ops:
  7.2 6.5 %collective-permute-start.1 = (bf16[512,768]{1,0:T(8,128)(2,1)}, bf16[512,768]{1,0:T(8,128)(2,1)S(1)}, u32[]{:S(2)}, u32[]{:S(2)}) collective-permute-start(bf16[512,768]{1,0:T(8,128)(2,1)} %refs_0_.1), channel_id=1, source_target_pairs={{0,7},{1,0},{2,1},{3,2},{4,3},{5,4},{6,5},{7,6},{8,15},{9,8},{10,9... | collective-permute-start | bytes 2359304 | tf_op jit(solution)/shard_map/ppermute | solution.py:409
  16.2 3.0 %collective-permute-start.4 = (bf16[400,512]{1,0:T(8,128)(2,1)S(1)}, bf16[400,512]{1,0:T(8,128)(2,1)S(1)}, u32[]{:S(2)}, u32[]{:S(2)}) collective-permute-start(bf16[400,512]{1,0:T(8,128)(2,1)S(1)} %get-tuple-element.61.a.refs_0_), channel_id=1, source_target_pairs={{0,16},{1,17},{2,18},{3,19},{4,20},{5,21},{6,22},{7,23},{8,24},{9,... | collective-permute-start | bytes 1228808 | tf_op jit(solution)/shard_map/ppermute | solution.py:423
  25.4 4.8 %pack.1 = (bf16[8,256,384]{2,1,0:T(8,128)(2,1)S(1)}, bf16[4,256,384]{2,1,0:T(8,128)(2,1)}, bf16[4,256,384]{2,1,0:T(8,128)(2,1)}, bf16[4,256,384]{2,1,0:T(8,128)(2,1)}) custom-call(s32[1]{0:T(128)} %bitcast.me, s32[1]{0:T(128)} %bitcast.2.d, s32[128]{0:T(128)S(1)} %copy-done.20, s32[128]{0:T(128)S(1)} %copy-done.18, s32[1]{0:T(128)S(6)} %copy.8.count, ...), custom_call_target="tpu_custom_call" | custom-call | bytes 7340032 | tf_op jit(solution)/shard_map/pack/pallas_call | solution.py:111
  31.4 6.7 %collective-permute-done.3.c.refs_2_ = bf16[400,512]{1,0:T(8,128)(2,1)} collective-permute-done((bf16[400,512]{1,0:T(8,128)(2,1)S(1)}, bf16[400,512]{1,0:T(8,128)(2,1)}, u32[]{:S(2)}, u32[]{:S(2)}) %collective-permute-start.3) | collective-permute-done | bytes 409632 | tf_op jit(solution)/shard_map/ppermute | solution.py:423
  38.2 2.7 %collective-permute-start.6 = (bf16[512,768]{1,0:T(8,128)(2,1)S(1)}, bf16[512,768]{1,0:T(8,128)(2,1)}, u32[]{:S(2)}, u32[]{:S(2)}) collective-permute-start(bf16[512,768]{1,0:T(8,128)(2,1)S(1)} %collective-permute-done.1.refs_5_.refs_1_), channel_id=1, source_target_pairs={{0,7},{1,0},{2,1},{3,2},{4,3},{5,4},{6,5},{7,6},{8,15},{9,8},{10,9... | collective-permute-start | bytes 2359304 | tf_op jit(solution)/shard_map/ppermute | solution.py:409
  40.9 2.7 %collective-permute-start.9 = (bf16[4,256,384]{2,1,0:T(8,128)(2,1)}, bf16[4,256,384]{2,1,0:T(8,128)(2,1)}, u32[]{:S(2)}, u32[]{:S(2)}) collective-permute-start(bf16[4,256,384]{2,1,0:T(8,128)(2,1)} %get-tuple-element.74), channel_id=1, source_target_pairs={{0,24},{1,25},{2,26},{3,27},{4,28},{5,29},{6,30},{7,31},{8,0},{9,1... | collective-permute-start | bytes 2359304 | tf_op jit(solution)/shard_map/ppermute | solution.py:429
  46.1 11.6 %collective-permute-done.5.refs_8_.refs_4_ = bf16[512,768]{1,0:T(8,128)(2,1)S(1)} collective-permute-done((bf16[512,768]{1,0:T(8,128)(2,1)S(1)}, bf16[512,768]{1,0:T(8,128)(2,1)S(1)}, u32[]{:S(2)}, u32[]{:S(2)}) %collective-permute-start.5) | collective-permute-done | bytes 786464 | tf_op jit(solution)/shard_map/ppermute | solution.py:409
  57.7 2.7 %collective-permute-start.8 = (bf16[512,768]{1,0:T(8,128)(2,1)}, bf16[512,768]{1,0:T(8,128)(2,1)}, u32[]{:S(2)}, u32[]{:S(2)}) collective-permute-start(bf16[512,768]{1,0:T(8,128)(2,1)} %collective-permute-done.6.refs_7_.refs_3_), channel_id=1, source_target_pairs={{0,7},{1,0},{2,1},{3,2},{4,3},{5,4},{6,5},{7,6},{8,15},{9,8},{10,9... | collective-permute-start | bytes 2359304 | tf_op jit(solution)/shard_map/ppermute | solution.py:409
  63.1 3.9 %early.1 = f32[384,5120]{1,0:T(8,128)S(1)} custom-call(s32[1]{0:T(128)} %bitcast.me, s32[4,128]{1,0:T(4,128)S(1)} %copy-done.13, bf16[400,512]{1,0:T(8,128)(2,1)S(1)} %copy-done.4, bf16[400,512]{1,0:T(8,128)(2,1)} %collective-permute-done.2.b.refs_1_, bf16[400,512]{1,0:T(8,128)(2,1)} %collective-permute-done.3.c.refs_2_, bf16[400,512]{1,0:T(8,128)(2,1)S(1)} %copy-done.7, ...), custom_call_target="tpu_custom_call" | custom-call | flops 2013265920 | bytes 13369344 | tf_op jit(solution)/shard_map/early/pallas_call | solution.py:151
  67.0 3.1 %copy-done = f32[384,5120]{1,0:T(8,128)} copy-done((f32[384,5120]{1,0:T(8,128)}, f32[384,5120]{1,0:T(8,128)S(1)}, u32[]{:S(2)}) %copy-start) | copy-done | bytes 7864344
  70.1 8.6 %collective-permute-done.11 = bf16[4,256,384]{2,1,0:T(8,128)(2,1)} collective-permute-done((bf16[4,256,384]{2,1,0:T(8,128)(2,1)}, bf16[4,256,384]{2,1,0:T(8,128)(2,1)}, u32[]{:S(2)}, u32[]{:S(2)}) %collective-permute-start.11) | collective-permute-done | bytes 786464 | tf_op jit(solution)/shard_map/ppermute | solution.py:429
  80.8 3.4 %collective-permute-start.14 = (bf16[3,4,256,384]{3,2,1,0:T(8,128)(2,1)S(1)}, bf16[3,4,256,384]{3,2,1,0:T(8,128)(2,1)S(1)}, u32[]{:S(2)}, u32[]{:S(2)}) collective-permute-start(bf16[3,4,256,384]{3,2,1,0:T(8,128)(2,1)S(1)} %pad_maximum_fusion.near), channel_id=1, source_target_pairs={{0,32},{32,0},{64,96},{96,64},{128,160},{160,128},{192,224},{224,1... | collective-permute-start | bytes 7077896 | tf_op jit(solution)/shard_map/ppermute | solution.py:412
  88.4 6.5 %inputs.1 = (f32[512,384]{1,0:T(8,128)S(1)}, f32[512,384]{1,0:T(8,128)S(1)}, f32[512,384]{1,0:T(8,128)S(1)}, f32[512,384]{1,0:T(8,128)S(1)}, bf16[4,1,256,384]{3,2,1,0:T(8,128)(2,1)S(1)}) custom-call(s32[1]{0:T(128)} %bitcast.me, s32[1]{0:T(128)} %bitcast.2.d, s32[4,128]{1,0:T(4,128)S(1)} %copy-done.14, bf16[8,256,384]{2,1,0:T(8,128)(2,1)S(1)} %copy-done.10, ...), custom_call_target="tpu_custom_call" | custom-call | flops 2818572288 | bytes 10485760 | tf_op jit(solution)/shard_map/inputs/pallas_call | solution.py:223
  94.9 2.3 %collective-permute-done.13.refs_1_.refs_7_ = bf16[256,768]{1,0:T(8,128)(2,1)S(1)} collective-permute-done((bf16[256,768]{1,0:T(8,128)(2,1)S(1)}, bf16[256,768]{1,0:T(8,128)(2,1)S(1)}, u32[]{:S(2)}, u32[]{:S(2)}) %collective-permute-start.13) | collective-permute-done | bytes 393248 | tf_op jit(solution)/shard_map/ppermute | solution.py:409
  100.8 3.3 %late.1 = (f32[192,3072]{1,0:T(8,128)S(1)}, f32[192,3072]{1,0:T(8,128)S(1)}) custom-call(s32[1]{0:T(128)} %bitcast.me, s32[1]{0:T(128)} %bitcast.2.d, s32[4,128]{1,0:T(4,128)S(1)} %copy-done.14, bf16[400,512]{1,0:T(8,128)(2,1)S(1)} %copy-done.5, bf16[400,512]{1,0:T(8,128)(2,1)} %collective-permute-done.2.b.refs_1_, ...), custom_call_target="tpu_custom_call" | custom-call | flops 1207959552 | bytes 9437184 | tf_op jit(solution)/shard_map/late/pallas_call | solution.py:186
  105.3 2.7 %collective-permute-start.17 = (f32[256,384]{1,0:T(8,128)S(1)}, f32[256,384]{1,0:T(8,128)S(1)}, u32[]{:S(2)}, u32[]{:S(2)}) collective-permute-start(f32[256,384]{1,0:T(8,128)S(1)} %get-tuple-element.110), channel_id=1, source_target_pairs={{0,24},{1,25},{2,26},{3,27},{4,28},{5,29},{6,30},{7,31},{8,0},{9,1... | collective-permute-start | bytes 1179656 | tf_op jit(solution)/shard_map/ppermute | solution.py:449
  110.4 6.8 %collective-permute-done.16.lo = f32[256,384]{1,0:T(8,128)S(1)} collective-permute-done((f32[256,384]{1,0:T(8,128)S(1)}, f32[256,384]{1,0:T(8,128)S(1)}, u32[]{:S(2)}, u32[]{:S(2)}) %collective-permute-start.16) | collective-permute-done | bytes 393248 | tf_op jit(solution)/shard_map/ppermute | solution.py:449
  118.6 2.7 %collective-permute-start.19 = (f32[512,384]{1,0:T(8,128)}, f32[512,384]{1,0:T(8,128)}, u32[]{:S(2)}, u32[]{:S(2)}) collective-permute-start(f32[512,384]{1,0:T(8,128)} %get-tuple-element.112), channel_id=1, source_target_pairs={{0,24},{1,25},{2,26},{3,27},{4,28},{5,29},{6,30},{7,31},{8,0},{9,1... | collective-permute-start | bytes 2359304 | tf_op jit(solution)/shard_map/ppermute | solution.py:456
  121.3 2.4 %collective-permute-start.22 = (f16[48,3200]{1,0:T(8,128)(2,1)S(1)}, f16[48,3200]{1,0:T(8,128)(2,1)S(1)}, u32[]{:S(2)}, u32[]{:S(2)}) collective-permute-start(f16[48,3200]{1,0:T(8,128)(2,1)S(1)} %convert_element_type.41), channel_id=1, source_target_pairs={{0,192},{32,224},{64,0},{96,32},{128,64},{160,96},{192,128},{224,1... | collective-permute-start | bytes 921608 | tf_op jit(solution)/shard_map/ppermute | solution.py:418
  124.8 8.3 %collective-permute-done.22 = f16[48,3200]{1,0:T(8,128)(2,1)S(1)} collective-permute-done((f16[48,3200]{1,0:T(8,128)(2,1)S(1)}, f16[48,3200]{1,0:T(8,128)(2,1)S(1)}, u32[]{:S(2)}, u32[]{:S(2)}) %collective-permute-start.22) | collective-permute-done | bytes 307232 | tf_op jit(solution)/shard_map/ppermute | solution.py:418
  135.3 6.7 %collective-permute-done.20 = f16[48,3200]{1,0:T(8,128)(2,1)S(1)} collective-permute-done((f16[48,3200]{1,0:T(8,128)(2,1)S(1)}, f16[48,3200]{1,0:T(8,128)(2,1)S(1)}, u32[]{:S(2)}, u32[]{:S(2)}) %collective-permute-start.20) | collective-permute-done | bytes 307232 | tf_op jit(solution)/shard_map/ppermute | solution.py:418
  143.9 2.8 %collective-permute-start.25 = (f16[48,2176]{1,0:T(8,128)(2,1)S(1)}, f16[48,2176]{1,0:T(8,128)(2,1)S(1)}, u32[]{:S(2)}, u32[]{:S(2)}) collective-permute-start(f16[48,2176]{1,0:T(8,128)(2,1)S(1)} %convert_element_type.50), channel_id=1, source_target_pairs={{0,16},{1,17},{2,18},{3,19},{4,20},{5,21},{6,22},{7,23},{8,24},{9,... | collective-permute-start | bytes 626696 | tf_op jit(solution)/shard_map/ppermute | solution.py:415
  151.2 4.4 %collective-permute-done.24 = f16[48,2176]{1,0:T(8,128)(2,1)S(1)} collective-permute-done((f16[48,2176]{1,0:T(8,128)(2,1)S(1)}, f16[48,2176]{1,0:T(8,128)(2,1)S(1)}, u32[]{:S(2)}, u32[]{:S(2)}) %collective-permute-start.24) | collective-permute-done | bytes 208928 | tf_op jit(solution)/shard_map/ppermute | solution.py:415
  156.1 3.1 %slots.1 = f32[128,16,128]{2,1,0:T(8,128)} custom-call(s32[1]{0:T(128)} %bitcast.me, s32[128]{0:T(128)S(1)} %copy-done.21, s32[128]{0:T(128)S(1)} %copy-done.19, s32[1]{0:T(128)S(6)} %copy.8.count, s32[8,128]{1,0:T(8,128)S(1)} %copy-done.16, f32[48,2048]{1,0:T(8,128)S(1)} %get-tuple-element.116.refs_0_, f32[48,2176]{1,0:T(8,128)S(1)} %convert_element_type.47.refs_1_, ...), custom_call_target="tpu_custom_call" | custom-call | bytes 5242880 | tf_op jit(solution)/shard_map/slots/pallas_call | solution.py:368
  (102 shorter events, 39.3 us)
Async XLA Ops:
  7.2 134.9 %reduce-scatter.2.cloned.1.call-start = ((), (), s32[]{:S(2)}) async-start(), calls=%async_computation.1 | async-start | bytes 8847360 | tf_op jit(solution)/shard_map/reduce_scatter | solution.py:438
  7.2 30.9 %collective-permute-start.1 = (bf16[512,768]{1,0:T(8,128)(2,1)}, bf16[512,768]{1,0:T(8,128)(2,1)S(1)}, u32[]{:S(2)}, u32[]{:S(2)}) collective-permute-start(bf16[512,768]{1,0:T(8,128)(2,1)} %refs_0_.1), channel_id=1, source_target_pairs={{0,7},{1,0},{2,1},{3,2},{4,3},{5,4},{6,5},{7,6},{8,15},{9,8},{10,9... | collective-permute-start | bytes 2359304 | tf_op jit(solution)/shard_map/ppermute | solution.py:409
  13.7 24.4 %collective-permute-start = (bf16[512,768]{1,0:T(8,128)(2,1)}, bf16[512,768]{1,0:T(8,128)(2,1)S(1)}, u32[]{:S(2)}, u32[]{:S(2)}) collective-permute-start(bf16[512,768]{1,0:T(8,128)(2,1)} %refs_0_.1), channel_id=1, source_target_pairs={{0,1},{1,2},{2,3},{3,4},{4,5},{5,6},{6,7},{7,0},{8,9},{9,10},{10,1... | collective-permute-start | bytes 2359304 | tf_op jit(solution)/shard_map/ppermute | solution.py:409
  16.2 15.2 %collective-permute-start.4 = (bf16[400,512]{1,0:T(8,128)(2,1)S(1)}, bf16[400,512]{1,0:T(8,128)(2,1)S(1)}, u32[]{:S(2)}, u32[]{:S(2)}) collective-permute-start(bf16[400,512]{1,0:T(8,128)(2,1)S(1)} %get-tuple-element.61.a.refs_0_), channel_id=1, source_target_pairs={{0,16},{1,17},{2,18},{3,19},{4,20},{5,21},{6,22},{7,23},{8,24},{9,... | collective-permute-start | bytes 1228808 | tf_op jit(solution)/shard_map/ppermute | solution.py:423
  19.2 18.9 %collective-permute-start.3 = (bf16[400,512]{1,0:T(8,128)(2,1)S(1)}, bf16[400,512]{1,0:T(8,128)(2,1)}, u32[]{:S(2)}, u32[]{:S(2)}) collective-permute-start(bf16[400,512]{1,0:T(8,128)(2,1)S(1)} %get-tuple-element.61.a.refs_0_), channel_id=1, source_target_pairs={{0,8},{1,9},{2,10},{3,11},{4,12},{5,13},{6,14},{7,15},{8,16},{9,17... | collective-permute-start | bytes 1228808 | tf_op jit(solution)/shard_map/ppermute | solution.py:423
  19.6 18.5 %collective-permute-start.2 = (bf16[400,512]{1,0:T(8,128)(2,1)S(1)}, bf16[400,512]{1,0:T(8,128)(2,1)}, u32[]{:S(2)}, u32[]{:S(2)}) collective-permute-start(bf16[400,512]{1,0:T(8,128)(2,1)S(1)} %get-tuple-element.61.a.refs_0_), channel_id=1, source_target_pairs={{0,24},{1,25},{2,26},{3,27},{4,28},{5,29},{6,30},{7,31},{8,0},{9,1... | collective-permute-start | bytes 1228808 | tf_op jit(solution)/shard_map/ppermute | solution.py:423
  38.1 19.6 %collective-permute-start.5 = (bf16[512,768]{1,0:T(8,128)(2,1)S(1)}, bf16[512,768]{1,0:T(8,128)(2,1)S(1)}, u32[]{:S(2)}, u32[]{:S(2)}) collective-permute-start(bf16[512,768]{1,0:T(8,128)(2,1)S(1)} %collective-permute-done.refs_6_.refs_2_), channel_id=1, source_target_pairs={{0,1},{1,2},{2,3},{3,4},{4,5},{5,6},{6,7},{7,0},{8,9},{9,10},{10,1... | collective-permute-start | bytes 2359304 | tf_op jit(solution)/shard_map/ppermute | solution.py:409
  38.2 19.5 %collective-permute-start.6 = (bf16[512,768]{1,0:T(8,128)(2,1)S(1)}, bf16[512,768]{1,0:T(8,128)(2,1)}, u32[]{:S(2)}, u32[]{:S(2)}) collective-permute-start(bf16[512,768]{1,0:T(8,128)(2,1)S(1)} %collective-permute-done.1.refs_5_.refs_1_), channel_id=1, source_target_pairs={{0,7},{1,0},{2,1},{3,2},{4,3},{5,4},{6,5},{7,6},{8,15},{9,8},{10,9... | collective-permute-start | bytes 2359304 | tf_op jit(solution)/shard_map/ppermute | solution.py:409
  40.9 29.2 %collective-permute-start.9 = (bf16[4,256,384]{2,1,0:T(8,128)(2,1)}, bf16[4,256,384]{2,1,0:T(8,128)(2,1)}, u32[]{:S(2)}, u32[]{:S(2)}) collective-permute-start(bf16[4,256,384]{2,1,0:T(8,128)(2,1)} %get-tuple-element.74), channel_id=1, source_target_pairs={{0,24},{1,25},{2,26},{3,27},{4,28},{5,29},{6,30},{7,31},{8,0},{9,1... | collective-permute-start | bytes 2359304 | tf_op jit(solution)/shard_map/ppermute | solution.py:429
  43.7 26.4 %collective-permute-start.10 = (bf16[4,256,384]{2,1,0:T(8,128)(2,1)}, bf16[4,256,384]{2,1,0:T(8,128)(2,1)}, u32[]{:S(2)}, u32[]{:S(2)}) collective-permute-start(bf16[4,256,384]{2,1,0:T(8,128)(2,1)} %get-tuple-element.75), channel_id=1, source_target_pairs={{0,8},{1,9},{2,10},{3,11},{4,12},{5,13},{6,14},{7,15},{8,16},{9,17... | collective-permute-start | bytes 2359304 | tf_op jit(solution)/shard_map/ppermute | solution.py:429
  43.7 35.0 %collective-permute-start.11 = (bf16[4,256,384]{2,1,0:T(8,128)(2,1)}, bf16[4,256,384]{2,1,0:T(8,128)(2,1)}, u32[]{:S(2)}, u32[]{:S(2)}) collective-permute-start(bf16[4,256,384]{2,1,0:T(8,128)(2,1)} %get-tuple-element.76), channel_id=1, source_target_pairs={{0,16},{1,17},{2,18},{3,19},{4,20},{5,21},{6,22},{7,23},{8,24},{9,... | collective-permute-start | bytes 2359304 | tf_op jit(solution)/shard_map/ppermute | solution.py:429
  57.7 21.0 %collective-permute-start.7 = (bf16[512,768]{1,0:T(8,128)(2,1)S(1)}, bf16[512,768]{1,0:T(8,128)(2,1)}, u32[]{:S(2)}, u32[]{:S(2)}) collective-permute-start(bf16[512,768]{1,0:T(8,128)(2,1)S(1)} %collective-permute-done.5.refs_8_.refs_4_), channel_id=1, source_target_pairs={{0,1},{1,2},{2,3},{3,4},{4,5},{5,6},{6,7},{7,0},{8,9},{9,10},{10,1... | collective-permute-start | bytes 2359304 | tf_op jit(solution)/shard_map/ppermute | solution.py:409
  57.7 21.0 %collective-permute-start.8 = (bf16[512,768]{1,0:T(8,128)(2,1)}, bf16[512,768]{1,0:T(8,128)(2,1)}, u32[]{:S(2)}, u32[]{:S(2)}) collective-permute-start(bf16[512,768]{1,0:T(8,128)(2,1)} %collective-permute-done.6.refs_7_.refs_3_), channel_id=1, source_target_pairs={{0,7},{1,0},{2,1},{3,2},{4,3},{5,4},{6,5},{7,6},{8,15},{9,8},{10,9... | collective-permute-start | bytes 2359304 | tf_op jit(solution)/shard_map/ppermute | solution.py:409
  86.2 10.9 %collective-permute-start.13 = (bf16[256,768]{1,0:T(8,128)(2,1)S(1)}, bf16[256,768]{1,0:T(8,128)(2,1)S(1)}, u32[]{:S(2)}, u32[]{:S(2)}) collective-permute-start(bf16[256,768]{1,0:T(8,128)(2,1)S(1)} %slice.7), channel_id=1, source_target_pairs={{0,7},{1,0},{2,1},{3,2},{4,3},{5,4},{6,5},{7,6},{8,15},{9,8},{10,9... | collective-permute-start | bytes 1179656 | tf_op jit(solution)/shard_map/ppermute | solution.py:409
  87.7 11.7 %collective-permute-start.12 = (bf16[256,768]{1,0:T(8,128)(2,1)S(1)}, bf16[256,768]{1,0:T(8,128)(2,1)S(1)}, u32[]{:S(2)}, u32[]{:S(2)}) collective-permute-start(bf16[256,768]{1,0:T(8,128)(2,1)S(1)} %slice.6), channel_id=1, source_target_pairs={{0,1},{1,2},{2,3},{3,4},{4,5},{5,6},{6,7},{7,0},{8,9},{9,10},{10,1... | collective-permute-start | bytes 1179656 | tf_op jit(solution)/shard_map/ppermute | solution.py:409
  105.3 12.0 %collective-permute-start.16 = (f32[256,384]{1,0:T(8,128)S(1)}, f32[256,384]{1,0:T(8,128)S(1)}, u32[]{:S(2)}, u32[]{:S(2)}) collective-permute-start(f32[256,384]{1,0:T(8,128)S(1)} %get-tuple-element.109), channel_id=1, source_target_pairs={{0,8},{1,9},{2,10},{3,11},{4,12},{5,13},{6,14},{7,15},{8,16},{9,17... | collective-permute-start | bytes 1179656 | tf_op jit(solution)/shard_map/ppermute | solution.py:449
  105.3 12.0 %collective-permute-start.17 = (f32[256,384]{1,0:T(8,128)S(1)}, f32[256,384]{1,0:T(8,128)S(1)}, u32[]{:S(2)}, u32[]{:S(2)}) collective-permute-start(f32[256,384]{1,0:T(8,128)S(1)} %get-tuple-element.110), channel_id=1, source_target_pairs={{0,24},{1,25},{2,26},{3,27},{4,28},{5,29},{6,30},{7,31},{8,0},{9,1... | collective-permute-start | bytes 1179656 | tf_op jit(solution)/shard_map/ppermute | solution.py:449
  118.6 29.6 %collective-permute-start.18 = (f32[512,384]{1,0:T(8,128)}, f32[512,384]{1,0:T(8,128)}, u32[]{:S(2)}, u32[]{:S(2)}) collective-permute-start(f32[512,384]{1,0:T(8,128)} %get-tuple-element.111), channel_id=1, source_target_pairs={{0,8},{1,9},{2,10},{3,11},{4,12},{5,13},{6,14},{7,15},{8,16},{9,17... | collective-permute-start | bytes 2359304 | tf_op jit(solution)/shard_map/ppermute | solution.py:456
  118.6 29.6 %collective-permute-start.19 = (f32[512,384]{1,0:T(8,128)}, f32[512,384]{1,0:T(8,128)}, u32[]{:S(2)}, u32[]{:S(2)}) collective-permute-start(f32[512,384]{1,0:T(8,128)} %get-tuple-element.112), channel_id=1, source_target_pairs={{0,24},{1,25},{2,26},{3,27},{4,28},{5,29},{6,30},{7,31},{8,0},{9,1... | collective-permute-start | bytes 2359304 | tf_op jit(solution)/shard_map/ppermute | solution.py:456
  121.3 11.9 %collective-permute-start.22 = (f16[48,3200]{1,0:T(8,128)(2,1)S(1)}, f16[48,3200]{1,0:T(8,128)(2,1)S(1)}, u32[]{:S(2)}, u32[]{:S(2)}) collective-permute-start(f16[48,3200]{1,0:T(8,128)(2,1)S(1)} %convert_element_type.41), channel_id=1, source_target_pairs={{0,192},{32,224},{64,0},{96,32},{128,64},{160,96},{192,128},{224,1... | collective-permute-start | bytes 921608 | tf_op jit(solution)/shard_map/ppermute | solution.py:418
  123.7 11.5 %collective-permute-start.21 = (f16[48,3200]{1,0:T(8,128)(2,1)S(1)}, f16[48,3200]{1,0:T(8,128)(2,1)S(1)}, u32[]{:S(2)}, u32[]{:S(2)}) collective-permute-start(f16[48,3200]{1,0:T(8,128)(2,1)S(1)} %convert_element_type.40), channel_id=1, source_target_pairs={{0,128},{32,160},{64,192},{96,224},{128,0},{160,32},{192,64},{224,... | collective-permute-start | bytes 921608 | tf_op jit(solution)/shard_map/ppermute | solution.py:418
  124.2 17.8 %collective-permute-start.20 = (f16[48,3200]{1,0:T(8,128)(2,1)S(1)}, f16[48,3200]{1,0:T(8,128)(2,1)S(1)}, u32[]{:S(2)}, u32[]{:S(2)}) collective-permute-start(f16[48,3200]{1,0:T(8,128)(2,1)S(1)} %convert_element_type.39), channel_id=1, source_target_pairs={{0,64},{32,96},{64,128},{96,160},{128,192},{160,224},{192,0},{224,... | collective-permute-start | bytes 921608 | tf_op jit(solution)/shard_map/ppermute | solution.py:418
  146.7 8.9 %collective-permute-start.24 = (f16[48,2176]{1,0:T(8,128)(2,1)S(1)}, f16[48,2176]{1,0:T(8,128)(2,1)S(1)}, u32[]{:S(2)}, u32[]{:S(2)}) collective-permute-start(f16[48,2176]{1,0:T(8,128)(2,1)S(1)} %convert_element_type.48), channel_id=1, source_target_pairs={{0,24},{1,25},{2,26},{3,27},{4,28},{5,29},{6,30},{7,31},{8,0},{9,1... | collective-permute-start | bytes 626696 | tf_op jit(solution)/shard_map/ppermute | solution.py:415
  148.2 7.8 %collective-permute-start.23 = (f16[48,2176]{1,0:T(8,128)(2,1)S(1)}, f16[48,2176]{1,0:T(8,128)(2,1)S(1)}, u32[]{:S(2)}, u32[]{:S(2)}) collective-permute-start(f16[48,2176]{1,0:T(8,128)(2,1)S(1)} %convert_element_type.46), channel_id=1, source_target_pairs={{0,8},{1,9},{2,10},{3,11},{4,12},{5,13},{6,14},{7,15},{8,16},{9,17... | collective-permute-start | bytes 626696 | tf_op jit(solution)/shard_map/ppermute | solution.py:415
  (25 other events, 184.8 us)
Sparse Core Ops, SparseCore 0:
  78.8 59.2 reduce-scatter.1
